TPU v7x, 32 devices: a whole 2x2x4 slice. The times are simulated.
32 devices in a mesh: sky: 4 (over y, x), tm: 4 (over z), fov: 2 (over core).
Axes of the slice: x: 2, y: 2, z: 4, core: 2. Of those that a mesh axis runs over, the one named last changes fastest.
Arguments:
- src_partials: float32 [65536, 5, 128], P(('sky', 'tm', 'fov')), may hold values from -0.375 to 0.375
- att_partials: float32 [65536, 4, 128], P(('sky', 'tm', 'fov')), may hold values from -0.3 to 0.3
- cal_partials: float32 [65536, 128], P(('sky', 'tm', 'fov')), may hold values from -0.6 to 0.6
- obs_phase: float32 [65536, 128], P(('sky', 'tm', 'fov')), may hold values from 0 to 1
- obs_residual: float32 [65536, 128], P(('sky', 'tm', 'fov')), may hold values from -6 to 6
- block_source: int32 [65536], P(('sky', 'tm', 'fov')), may hold values from 0 to 4095
- block_segment: int32 [65536], P(('sky', 'tm', 'fov')), may hold values from 0 to 511, as said below
- block_unit: int32 [65536], P(('sky', 'tm', 'fov')), may hold values from 0 to 524287, as said below
- live_blocks: int32 [32], P(('sky', 'tm', 'fov')), may hold values from 896 to 2048, as said below
Outputs:
- src_update: float32 [5, 16384], P(None, 'sky')
- att_update: float32 [4, 4, 512], P(None, 'tm', 'sky')
- cal_update: float32 [524288], P(('sky', 'tm', 'fov'))
Inputs may be any that keep to these rules, and one draw needn't show every extreme that they name: `block_segment`: only live blocks' segments matter. Of one device's live blocks at most 512 have segments of one sky index (s * 128 to (s + 1) * 128 - 1); for every tm and fov index some sky index s has exactly 512 such live blocks from every device of that tm and fov index. A device's live blocks are its first live_blocks blocks. `block_unit`: units fall into 32 ranges of 524288 / 32 units each (range r is the units of output shard r). Of one device's blocks, live or not, at most 128 have units of one range; on every device some range has exactly 128.
All inputs are finite; a program needn't handle non-finite values.
Results may differ from a plain program's by a relative error of at most 0.00011.
Values sent between devices are 32-bit elements; how exact they have to be, the bound alone decides.
A program may use at most 128 MiB of HBM per device.

v0:
```python
import jax
import jax.numpy as jnp
from jax import lax
from jax.sharding import PartitionSpec as P

SRC_DEV = 4096
SEG_DEV = 128
CAL = 524288


index_pairs = [(i, j) for i in range(5) for j in range(i, 5)]


def spline_basis(phase):
    rest = 1.0 - phase
    square = phase * phase
    cubed = square * phase
    return jnp.stack(
        [
            rest * rest * rest / 6.0,
            (3.0 * cubed - 6.0 * square + 4.0) / 6.0,
            (-3.0 * cubed + 3.0 * square + 3.0 * phase + 1.0) / 6.0,
            cubed / 6.0,
        ],
        axis=1,
    )


def spline_products(residual, partials, phase):
    basis = spline_basis(phase)
    weighted = partials * residual[:, None, :]
    right_side = jnp.einsum("bjo,bco->bjc", basis, weighted, precision=lax.Precision.HIGHEST)
    diag_part = jnp.einsum(
        "bjo,bco->bjc", basis * basis, partials * partials, precision=lax.Precision.HIGHEST
    )
    return jnp.concatenate([right_side, diag_part], axis=2)


def block_products(partials, residual, live_mask):
    products = jnp.stack(
        [jnp.sum(partials[:, i, :] * partials[:, j, :], axis=1) for i, j in index_pairs], axis=1
    )
    right_side = jnp.sum(partials * residual[:, None, :], axis=2)
    return (products * live_mask[:, None], right_side * live_mask[:, None])


def solve_normals(packed, right_side):
    matrix = {}
    for position, (i, j) in enumerate(index_pairs):
        matrix[i, j] = packed[position] + (1.0 if i == j else 0.0)
    factor = {}
    for i in range(5):
        for j in range(i + 1):
            running = matrix[j, i]
            for k in range(j):
                running = running - factor[i, k] * factor[j, k]
            if i == j:
                factor[i, i] = jnp.sqrt(running)
            else:
                factor[i, j] = running / factor[j, j]
    forward = []
    for i in range(5):
        running = right_side[i]
        for k in range(i):
            running = running - factor[i, k] * forward[k]
        forward.append(running / factor[i, i])
    result = [forward[0]] * 5
    for i in reversed(range(5)):
        running = forward[i]
        for k in range(i + 1, 5):
            running = running - factor[k, i] * result[k]
        result[i] = running / factor[i, i]
    return jnp.stack(result)


def shards(
    src_partials,
    att_partials,
    cal_partials,
    obs_phase,
    obs_residual,
    block_source,
    block_segment,
    block_unit,
    live_blocks,
):
    blocks = src_partials.shape[0]
    live_mask = (jnp.arange(blocks, dtype=jnp.int32) < live_blocks[0]).astype(jnp.float32)
    products, right_side = block_products(src_partials, obs_residual, live_mask)
    normals = jax.ops.segment_sum(products, block_source, num_segments=SRC_DEV).T
    source_right = jax.ops.segment_sum(right_side, block_source, num_segments=SRC_DEV).T
    normals, source_right = lax.psum((normals, source_right), ("tm", "fov"))
    src_update = solve_normals(normals, source_right)
    chosen = src_update[:, block_source].T
    residual = obs_residual - jnp.sum(src_partials * chosen[:, :, None], axis=1)
    sky_count = lax.axis_size("sky")
    arc_length = SEG_DEV * sky_count
    values = spline_products(residual, att_partials, obs_phase) * live_mask[:, None, None]
    offsets = block_segment[:, None] + jnp.arange(4, dtype=jnp.int32)[None, :]
    knot_index = jnp.where((offsets < arc_length) & (live_mask[:, None] > 0.0), offsets, arc_length)
    dense_knots = jax.ops.segment_sum(
        values.reshape(-1, 8), knot_index.reshape(-1), num_segments=arc_length + 1
    )[:arc_length].T
    knots = lax.psum_scatter(dense_knots, "sky", scatter_dimension=1, tiled=True)
    knots = lax.psum(knots, "fov")
    attitude = knots[:4] / (1.0 + knots[4:])
    att_update = attitude.reshape(4, 1, attitude.shape[1])
    block_right = jnp.sum(cal_partials * residual, axis=1) * live_mask
    block_diag = jnp.sum(cal_partials * cal_partials, axis=1) * live_mask
    device_count = lax.axis_size(("sky", "tm", "fov"))
    share = CAL // device_count
    unit_right = jax.ops.segment_sum(block_right, block_unit, num_segments=CAL)
    unit_diag = jax.ops.segment_sum(block_diag, block_unit, num_segments=CAL)
    whole_right, whole_diag = lax.psum((unit_right, unit_diag), ("sky", "tm", "fov"))
    start = lax.axis_index(("sky", "tm", "fov")) * share
    mine_right = lax.dynamic_slice_in_dim(whole_right, start, share)
    mine_diag = lax.dynamic_slice_in_dim(whole_diag, start, share)
    cal_update = mine_right / (1.0 + mine_diag)
    return (src_update, att_update, cal_update)


def solution(mesh):
    return jax.shard_map(
        shards,
        mesh=mesh,
        in_specs=(
            P(("sky", "tm", "fov"), None, None),
            P(("sky", "tm", "fov"), None, None),
            P(("sky", "tm", "fov"), None),
            P(("sky", "tm", "fov"), None),
            P(("sky", "tm", "fov"), None),
            P(("sky", "tm", "fov")),
            P(("sky", "tm", "fov")),
            P(("sky", "tm", "fov")),
            P(("sky", "tm", "fov")),
        ),
        out_specs=(P(None, "sky"), P(None, "tm", "sky"), P(("sky", "tm", "fov"))),
        check_vma=False,
    )
```

profile of v0, /device:TPU:0, one launch (start us, length us, event | category | flops | bytes accessed | tf_op | source)
XLA Modules:
  0.0 393.3 jit_solution(2789168913030656194)
XLA Ops:
  7.2 6.6 %multiply_reduce_fusion.14 = (f32[2048]{0:T(1024)S(1)}, f32[2048]{0:T(1024)S(1)}, f32[2048]{0:T(1024)S(1)}, f32[2048]{0:T(1024)S(1)}, f32[2048]{0:T(1024)S(1)}, ...) fusion(f32[2048,5,128]{2,0,1:T(8,128)} %param.9), kind=kLoop, calls=%fused_computation.44 | loop fusion | flops 7833600 | bytes 5365760 | tf_op jit(solution)/shard_map/reduce_sum | solution.py:41
  16.2 12.3 %scatter_custom_fusion.1 = f32[4096,15]{1,0:T(8,128)S(1)} fusion(s32[2048]{0:T(1024)S(1)} %copy-done.12, f32[2048,15]{1,0:T(8,128)} %copy.78, f32[]{:T(128)} %constant.16.clone.1), kind=kCustom, calls=%fused_computation.49 | custom fusion | flops 30720 | bytes 246272 | tf_op jit(solution)/shard_map/scatter-add | solution.py:90
  29.9 3.9 multiply_reduce_fusion.1
  35.2 12.3 %scatter_custom_fusion = f32[4096,5]{1,0:T(8,128)S(1)} fusion(s32[2048]{0:T(1024)S(1)} %copy-done.12, f32[2048,5]{1,0:T(8,128)} %copy.76, f32[]{:T(128)} %constant.16.clone.1), kind=kCustom, calls=%fused_computation.51 | custom fusion | flops 10240 | bytes 82432 | tf_op jit(solution)/shard_map/scatter-add | solution.py:91
  49.1 2.0 fusion.13
  51.6 18.1 %fusion = f32[2048,4,4]{2,1,0:T(4,128)} fusion(f32[2048,4,128]{2,1,0:T(4,128)S(1)} %copy-done.13, f32[2048,1,128]{2,1,0:T(1,128)S(1)} %bitcast.46, f32[2048,1,128]{2,1,0:T(1,128)S(1)} %bitcast.44, f32[2048,1,128]{2,1,0:T(1,128)S(1)} %bitcast.42, f32[2048,1,128]{2,1,0:T(1,128)S(1)} %bitcast.40), kind=kOutput, calls=%fused_computation.9 | convolution fusion | flops 55574528 | bytes 8519680 | tf_op jit(solution)/shard_map/bjo,bco->bjc/dot_general | solution.py:33
  69.8 2.9 copy.86
  75.9 31.4 %all-reduce.7.cloned.1.call-done = (f32[15,4096]{1,0:T(8,128)}, f32[5,4096]{1,0:T(8,128)}) async-done(((f32[15,4096]{1,0:T(8,128)}, f32[5,4096]{1,0:T(8,128)}), (f32[15,4096]{1,0:T(8,128)}, f32[5,4096]{1,0:T(8,128)})) %all-reduce.7.cloned.1.call-update) | async-done | bytes 327696 | tf_op jit(solution)/shard_map/psum | solution.py:92
  107.3 2.4 fusion.53
  109.7 1.7 fusion.54
  111.4 1.7 subtract_divide_fusion
  113.9 7.6 %gather_fusion = f32[2048,5]{1,0:T(8,128)} fusion(f32[5,4096]{0,1:T(8,128)S(1)} %copy.83, s32[2048]{0:T(1024)S(1)} %fusion.55), kind=kCustom, calls=%fused_computation | custom fusion | bytes 90112 | tf_op jit(solution)/shard_map/gather | solution.py:94
  121.4 1.6 copy.84
  123.1 13.6 %multiply_reduce_fusion = f32[2048,128]{1,0:T(8,128)S(1)} fusion(f32[2048,5,128]{2,0,1:T(8,128)} %param.9, f32[2048,5]{0,1:T(8,128)S(1)} %copy.84), kind=kLoop, calls=%fused_computation.6 | loop fusion | flops 2359296 | bytes 6332416 | tf_op jit(solution)/shard_map/reduce_sum | solution.py:95
  137.5 19.9 %fusion.3 = f32[2048,4,4]{2,1,0:T(4,128)} fusion(f32[2048,4,128]{2,1,0:T(4,128)S(1)} %copy-done.14, f32[2048,128]{1,0:T(8,128)S(1)} %get-tuple-element.42, f32[2048,1,128]{2,1,0:T(1,128)S(1)} %bitcast.47, f32[2048,1,128]{2,1,0:T(1,128)S(1)} %bitcast.45, f32[2048,1,128]{2,1,0:T(1,128)S(1)} %bitcast.43, f32[2048,1,128]{2,1,0:T(1,128)S(1)} %bitcast.41), kind=kOutput, calls=%fused_computation.12 | convolution fusion | flops 54525952 | bytes 9568256 | tf_op jit(solution)/shard_map/bjo,bco->bjc/dot_general | solution.py:32
  157.4 2.8 copy.85
  160.3 2.6 copy.87
  162.9 44.4 %scatter_custom_fusion.2 = f32[513,8]{1,0:T(8,128)S(1)} fusion(s32[8192]{0:T(1024)S(1)} %bitcast.65, f32[8192,8]{1,0:T(8,128)} %copy.87, f32[]{:T(128)} %constant.16.clone.1), kind=kCustom, calls=%fused_computation.56 | custom fusion | flops 65536 | bytes 16928 | tf_op jit(solution)/shard_map/scatter-add | solution.py:101
  208.1 12.8 %scatter_custom_fusion.3 = f32[524288]{0:T(1024)} fusion(s32[2048]{0:T(1024)} %param.16, f32[2048]{0:T(1024)S(1)} %get-tuple-element.79, f32[]{:T(128)} %constant.16.clone.1), kind=kCustom, calls=%fused_computation.31 | custom fusion | flops 2048 | bytes 2097664 | tf_op jit(solution)/shard_map/scatter-add | solution.py:112
  220.9 12.8 %scatter_custom_fusion.4 = f32[524288]{0:T(1024)} fusion(s32[2048]{0:T(1024)} %param.16, f32[2048]{0:T(1024)S(1)} %get-tuple-element.78, f32[]{:T(128)} %constant.16.clone.1), kind=kCustom, calls=%fused_computation.29 | custom fusion | flops 2048 | bytes 2097664 | tf_op jit(solution)/shard_map/scatter-add | solution.py:113
  233.8 3.5 reduce-scatter.2.cloned.1.call-done
  237.2 4.2 %psum.37 = f32[8,128]{0,1:T(8,128)S(1)} all-reduce(f32[8,128]{0,1:T(8,128)} %reduce-scatter.2.cloned.1.call-done), channel_id=1, replica_groups=mesh['sky'=4,'tm'=4,'fov'=2] {'fov'}, use_global_device_ids=true, to_apply=%region_23.24 | all-reduce | flops 1024 | bytes 8192 | tf_op jit(solution)/shard_map/psum | solution.py:105
  242.2 142.9 %all-reduce.5.cloned.1.call-done = (f32[524288]{0:T(1024)}, f32[524288]{0:T(1024)}) async-done(((f32[524288]{0:T(1024)}, f32[524288]{0:T(1024)}), (f32[524288]{0:T(1024)}, f32[524288]{0:T(1024)})) %all-reduce.5.cloned.1.call-update) | async-done | bytes 4194320 | tf_op jit(solution)/shard_map/psum | solution.py:114
  385.0 1.5 add_divide_fusion
  (61 shorter events, 12.7 us)
Async XLA Ops:
  7.2 9.0 %copy-start.12 = (s32[2048]{0:T(1024)S(1)}, s32[2048]{0:T(1024)}, u32[]{:S(2)}) copy-start(s32[2048]{0:T(1024)} %param.14) | copy-start | bytes 24580
  7.2 100.1 %all-reduce.7.cloned.1.call-start = ((), (), s32[]{:S(2)}) async-start(), calls=%async_computation.3 | async-start | bytes 786432 | tf_op jit(solution)/shard_map/psum | solution.py:92
  13.8 16.0 %copy-start = (f32[2048,128]{1,0:T(8,128)S(1)}, f32[2048,128]{1,0:T(8,128)}, u32[]{:S(2)}) copy-start(f32[2048,128]{1,0:T(8,128)} %param.13) | copy-start | bytes 3145732
  48.8 188.4 %reduce-scatter.2.cloned.1.call-start = ((), (), s32[]{:S(2)}) async-start(), calls=%async_computation.1 | async-start | bytes 327680 | tf_op jit(solution)/shard_map/reduce_scatter | solution.py:104
  49.1 2.5 copy-start.13
  51.1 18.6 %copy-start.1 = (f32[2048,128]{1,0:T(8,128)}, f32[2048,128]{1,0:T(8,128)S(1)}, u32[]{:S(2)}) copy-start(f32[2048,128]{1,0:T(8,128)S(1)} %get-tuple-element.74) | copy-start | bytes 3145732
  51.2 18.6 %copy-start.3 = (f32[2048,128]{1,0:T(8,128)}, f32[2048,128]{1,0:T(8,128)S(1)}, u32[]{:S(2)}) copy-start(f32[2048,128]{1,0:T(8,128)S(1)} %get-tuple-element.75) | copy-start | bytes 3145732
  51.2 18.6 %copy-start.5 = (f32[2048,128]{1,0:T(8,128)}, f32[2048,128]{1,0:T(8,128)S(1)}, u32[]{:S(2)}) copy-start(f32[2048,128]{1,0:T(8,128)S(1)} %get-tuple-element.76) | copy-start | bytes 3145732
  51.2 18.6 %copy-start.7 = (f32[2048,128]{1,0:T(8,128)}, f32[2048,128]{1,0:T(8,128)S(1)}, u32[]{:S(2)}) copy-start(f32[2048,128]{1,0:T(8,128)S(1)} %get-tuple-element.77) | copy-start | bytes 3145732
  69.8 5.0 %copy-start.11 = (s32[2048]{0:T(1024)S(1)}, s32[2048]{0:T(1024)}, u32[]{:S(2)}) copy-start(s32[2048]{0:T(1024)} %param.15) | copy-start | bytes 24580
  113.2 23.6 %copy-start.10 = (f32[5,4096]{1,0:T(8,128)}, f32[5,4096]{1,0:T(8,128)S(1)}, u32[]{:S(2)}) copy-start(f32[5,4096]{1,0:T(8,128)S(1)} %stack.87) | copy-start | bytes 245764
  121.4 15.3 %copy-start.9 = (f32[2048,128]{1,0:T(8,128)S(1)}, f32[2048,128]{1,0:T(8,128)}, u32[]{:S(2)}) copy-start(f32[2048,128]{1,0:T(8,128)} %param.11) | copy-start | bytes 3145732
  123.1 14.4 %copy-start.2 = (f32[2048,128]{1,0:T(8,128)S(1)}, f32[2048,128]{1,0:T(8,128)}, u32[]{:S(2)}) copy-start(f32[2048,128]{1,0:T(8,128)} %copy-done.1) | copy-start | bytes 3145732
  123.1 14.4 %copy-start.4 = (f32[2048,128]{1,0:T(8,128)S(1)}, f32[2048,128]{1,0:T(8,128)}, u32[]{:S(2)}) copy-start(f32[2048,128]{1,0:T(8,128)} %copy-done.3) | copy-start | bytes 3145732
  123.1 14.4 %copy-start.6 = (f32[2048,128]{1,0:T(8,128)S(1)}, f32[2048,128]{1,0:T(8,128)}, u32[]{:S(2)}) copy-start(f32[2048,128]{1,0:T(8,128)} %copy-done.5) | copy-start | bytes 3145732
  123.1 14.4 %copy-start.8 = (f32[2048,128]{1,0:T(8,128)S(1)}, f32[2048,128]{1,0:T(8,128)}, u32[]{:S(2)}) copy-start(f32[2048,128]{1,0:T(8,128)} %copy-done.7) | copy-start | bytes 3145732
  123.1 14.4 %copy-start.14 = (f32[2048,4,128]{2,1,0:T(4,128)S(1)}, f32[2048,4,128]{2,1,0:T(4,128)}, u32[]{:S(2)}) copy-start(f32[2048,4,128]{2,1,0:T(4,128)} %param.10) | copy-start | bytes 12582916
  208.0 177.0 %all-reduce.5.cloned.1.call-start = ((), (), s32[]{:S(2)}) async-start(), calls=%async_computation.2 | async-start | bytes 8388608 | tf_op jit(solution)/shard_map/psum | solution.py:114
Sparse Core Ops, SparseCore 0:
  48.9 58.3 all-reduce.6
  208.2 29.0 reduce-scatter.1
  242.9 142.0 all-reduce.4
where the time goes:
time: 398 us; the launch traced here: 393 us
  waiting for transfers between devices  178 us (45%)
  other arithmetic  129 us (32%)
  matrix products  38 us (10%)
  local copies, waits for them, and re-layouts  28.5 us (7%)
  between operations  15 us (4%)
  blocking collectives  4.19 us (1%)
    psum x1, waiting for transfers between devices, shards(): lax.psum((unit_right, unit_diag), ('sky', 'tm', 'fov'))  143 us
    scatter-add x1, other arithmetic, shards(): jax.ops.segment_sum(values.reshape(-1, 8), knot_index.reshape(-1), num_se...  44.4 us
    psum x1, waiting for transfers between devices, shards(): normals, source_right = lax.psum((normals, source_right), ('tm', 'fov'))  31.4 us
    dot_general x1, matrix products, spline_products(): jnp.einsum('bjo,bco->bjc', basis, weighted, precision=lax.Precision.HIGHEST)  19.9 us
    dot_general x1, matrix products, spline_products(): jnp.einsum('bjo,bco->bjc', basis * basis, partials * partials, precision=...  18.1 us
    reduce_sum x1, other arithmetic, shards(): residual = obs_residual - jnp.sum(src_partials * chosen[:, :, None], axis=1)  13.6 us
    scatter-add x1, other arithmetic, shards(): unit_right = jax.ops.segment_sum(block_right, block_unit, num_segments=CAL)  12.8 us
    scatter-add x1, other arithmetic, shards(): unit_diag = jax.ops.segment_sum(block_diag, block_unit, num_segments=CAL)  12.8 us
  transfers between devices with their start and end apart: 3, of which 3 were waited for; matrix products, arithmetic and copies ran while one was open for 13% of the time, Pallas kernels for 0%

commit v1 on v0

v1 whole, which is shorter than its diff:
```python
import functools

import jax
import jax.numpy as jnp
from jax import lax
from jax.experimental import pallas as pl
from jax.experimental.pallas import tpu as pltpu
from jax.sharding import PartitionSpec as P

SRC_DEV = 4096
SEG_DEV = 128
CAL = 524288
LANES = 128
LOW = 256
F32 = jnp.float32
BF16 = jnp.bfloat16
MESH = pl.DeviceIdType.MESH

index_pairs = [(i, j) for i in range(5) for j in range(i, 5)]
NT = (((1,), (1,)), ((), ()))
NN = (((1,), (0,)), ((), ()))


def split(values):
    first = values.astype(BF16).astype(F32)
    return first, values - first


def one_hot(rows, index):
    grid = lax.broadcasted_iota(jnp.int32, (rows, index.shape[1]), 0)
    return jnp.where(grid == index, 1.0, 0.0).astype(BF16)


def solve_rows(entries):
    matrix = {}
    for position, (i, j) in enumerate(index_pairs):
        matrix[i, j] = entries[position] + (1.0 if i == j else 0.0)
    right_side = entries[15:20]
    factor = {}
    inverse = []
    for j in range(5):
        running = matrix[j, j]
        for k in range(j):
            running = running - factor[j, k] * factor[j, k]
        inverse.append(1.0 / jnp.sqrt(running))
        for i in range(j + 1, 5):
            running = matrix[j, i]
            for k in range(j):
                running = running - factor[i, k] * factor[j, k]
            factor[i, j] = running * inverse[j]
    forward = []
    for i in range(5):
        running = right_side[i]
        for k in range(i):
            running = running - factor[i, k] * forward[k]
        forward.append(running * inverse[i])
    result = [None] * 5
    for i in reversed(range(5)):
        running = forward[i]
        for k in range(i + 1, 5):
            running = running - factor[k, i] * result[k]
        result[i] = running * inverse[i]
    return result


def fold(total):
    return jnp.sum(total, axis=0, keepdims=True)


def kernel(
    sizes,
    src_hbm,
    att_hbm,
    cal_hbm,
    phase_hbm,
    res_hbm,
    source_ref,
    segment_ref,
    unit_ref,
    live_ref,
    src_out,
    att_out,
    cal_out,
    src_in,
    att_in,
    cal_in,
    phase_in,
    res_in,
    src_t,
    att_t,
    basis_t,
    cal_t,
    sums,
    knot_sums,
    unit_sums,
    low_hot,
    spread,
    table,
    table_in,
    update,
    chosen,
    rank_row,
    slot_hot,
    knot_send,
    knot_in,
    unit_send,
    unit_in,
    chunk_sems,
    whole_sems,
    table_sems,
    update_sems,
    knot_sems,
    unit_sems,
):
    n_sky, n_tm, n_fov = sizes
    devices = n_sky * n_tm * n_fov
    blocks = res_hbm.shape[0]
    groups = blocks // LANES
    parts = n_tm * n_fov
    high = SRC_DEV // LOW
    per_part = high // parts
    plane = n_sky * n_fov
    share = CAL // devices
    unit_high = share // LANES

    sky = lax.axis_index("sky")
    tm = lax.axis_index("tm")
    fov = lax.axis_index("fov")
    me = (sky * n_tm + tm) * n_fov + fov
    part_me = tm * n_fov + fov
    plane_me = sky * n_fov + fov

    def any_peer(k):
        q = lax.rem(me + k, devices)
        return (
            lax.div(q, n_tm * n_fov),
            lax.rem(lax.div(q, n_fov), n_tm),
            lax.rem(q, n_fov),
        )

    barrier = pltpu.get_barrier_semaphore()
    for k in range(1, devices):
        pl.semaphore_signal(barrier, inc=1, device_id=any_peer(k), device_id_type=MESH)

    def chunk_copies(g):
        rows = pl.ds(pl.multiple_of(g * LANES, LANES), LANES)
        return (
            pltpu.make_async_copy(src_hbm.at[:, rows], src_in.at[:, rows], chunk_sems.at[0, g]),
            pltpu.make_async_copy(res_hbm.at[rows], res_in.at[rows], chunk_sems.at[1, g]),
        )

    whole_copies = [
        pltpu.make_async_copy(att_hbm, att_in, whole_sems.at[0]),
        pltpu.make_async_copy(cal_hbm, cal_in, whole_sems.at[1]),
        pltpu.make_async_copy(phase_hbm, phase_in, whole_sems.at[2]),
    ]

    def start_chunk(g, carry):
        for copy in chunk_copies(g):
            copy.start()
        return carry

    lax.fori_loop(0, groups, start_chunk, 0)
    for copy in whole_copies:
        copy.start()

    def source_sums(g, carry):
        for copy in chunk_copies(g):
            copy.wait()
        rows = pl.ds(pl.multiple_of(g * LANES, LANES), LANES)
        for c in range(5):
            src_t[g, c] = src_in[c, rows, :].T
        src_t[g, 5] = res_in[rows, :].T
        totals = None
        for t in range(LANES // 8):
            tile = pl.ds(t * 8, 8)
            a = [src_t[g, c, tile, :] for c in range(6)]
            terms = [a[i] * a[j] for i, j in index_pairs] + [a[i] * a[5] for i in range(5)]
            totals = terms if totals is None else [x + y for x, y in zip(totals, terms)]
        for q in range(20):
            sums[q : q + 1, rows] = fold(totals[q])
        return carry

    lax.fori_loop(0, groups, source_sums, 0)
    sums[20:24, :] = jnp.zeros((4, blocks), F32)

    live = lax.broadcasted_iota(jnp.int32, (1, blocks), 1) < live_ref[0]
    source = source_ref[...]
    source_high = source >> 8
    low_hot[...] = one_hot(LOW, source & (LOW - 1))
    pair = jnp.concatenate(split(jnp.where(live, sums[...], 0.0)), axis=0)
    for h in range(high):
        spread[48 * h : 48 * h + 48, :] = jnp.where(source_high == h, pair, 0.0).astype(BF16)
    placed = lax.dot_general(
        spread[: 48 * high, :], low_hot[...], NT, preferred_element_type=F32
    )
    for h in range(high):
        table[h // per_part, h % per_part] = (
            placed[48 * h : 48 * h + 24] + placed[48 * h + 24 : 48 * h + 48]
        )

    pl.semaphore_wait(barrier, devices - 1)

    table_copies = []
    for k in range(1, parts):
        p = lax.rem(part_me + k, parts)
        copy = pltpu.make_async_remote_copy(
            src_ref=table.at[p],
            dst_ref=table_in.at[k],
            send_sem=table_sems.at[0, k],
            recv_sem=table_sems.at[1, k],
            device_id=(sky, lax.div(p, n_fov), lax.rem(p, n_fov)),
            device_id_type=MESH,
        )
        copy.start()
        table_copies.append(copy)

    for copy in whole_copies:
        copy.wait()

    def fixed_sums(g, carry):
        rows = pl.ds(pl.multiple_of(g * LANES, LANES), LANES)
        for c in range(4):
            att_t[g, c] = att_in[rows, c, :].T
        cal_t[g] = cal_in[rows, :].T
        phase_t = phase_in[rows, :].T
        rest = 1.0 - phase_t
        square = phase_t * phase_t
        cubed = square * phase_t
        basis_t[g, 0] = rest * rest * rest * (1.0 / 6.0)
        basis_t[g, 1] = (3.0 * cubed - 6.0 * square + 4.0) * (1.0 / 6.0)
        basis_t[g, 2] = (-3.0 * cubed + 3.0 * square + 3.0 * phase_t + 1.0) * (1.0 / 6.0)
        basis_t[g, 3] = cubed * (1.0 / 6.0)
        totals = None
        for t in range(LANES // 8):
            tile = pl.ds(t * 8, 8)
            b = [basis_t[g, j, tile, :] for j in range(4)]
            h = [att_t[g, c, tile, :] for c in range(4)]
            b = [x * x for x in b]
            h = [x * x for x in h]
            u = cal_t[g, tile, :]
            terms = [b[j] * h[c] for j in range(4) for c in range(4)] + [u * u]
            totals = terms if totals is None else [x + y for x, y in zip(totals, terms)]
        for j in range(4):
            for c in range(4):
                q = j * 8 + 4 + c
                knot_sums[q : q + 1, rows] = fold(totals[j * 4 + c])
        unit_sums[1:2, rows] = fold(totals[16])
        return carry

    lax.fori_loop(0, groups, fixed_sums, 0)

    unit = unit_ref[...]
    owner = lax.div(unit, share)
    local = unit - owner * share
    row = lax.broadcasted_iota(jnp.int32, (LANES, 2 * LANES), 0)
    column = lax.broadcasted_iota(jnp.int32, (LANES, 2 * LANES), 1)
    ramp = jnp.where(row <= column, 1.0, 0.0).astype(BF16)
    before = jnp.zeros((devices, LANES), F32)
    for g in range(groups):
        cut = slice(g * LANES, (g + 1) * LANES)
        hot = lax.broadcasted_iota(jnp.int32, (devices, LANES), 0) == owner[:, cut]
        hot = jnp.where(hot, 1.0, 0.0)
        counts = lax.dot_general(hot.astype(BF16), ramp, NN, preferred_element_type=F32)
        rank_row[:, cut] = fold(hot * (counts[:, :LANES] + before)) - 1.0
        before = before + counts[:, LANES:]
    slot_hot[...] = one_hot(LANES, rank_row[...].astype(jnp.int32))

    for copy in table_copies:
        copy.wait_recv()
    for s in range(per_part):
        total = table[part_me, s]
        for k in range(1, parts):
            total = total + table_in[k, s]
        solved = solve_rows([total[q : q + 1] for q in range(20)])
        for c in range(5):
            update[part_me, s, c : c + 1, :] = solved[c]
        update[part_me, s, 5:8, :] = jnp.zeros((3, LOW), F32)

    update_copies = []
    for k in range(1, parts):
        p = lax.rem(part_me + k, parts)
        copy = pltpu.make_async_remote_copy(
            src_ref=update.at[part_me],
            dst_ref=update.at[part_me],
            send_sem=update_sems.at[0, k],
            recv_sem=update_sems.at[1, k],
            device_id=(sky, lax.div(p, n_fov), lax.rem(p, n_fov)),
            device_id_type=MESH,
        )
        copy.start()
        update_copies.append(copy)
    for k in range(1, parts):
        p = lax.rem(part_me + parts - k, parts)
        pltpu.make_async_remote_copy(
            src_ref=update.at[part_me],
            dst_ref=update.at[p],
            send_sem=update_sems.at[0, k],
            recv_sem=update_sems.at[1, k],
            device_id=(sky, lax.div(p, n_fov), lax.rem(p, n_fov)),
            device_id_type=MESH,
        ).wait_recv()

    pieces = []
    for h in range(high):
        piece = update[h // per_part, h % per_part]
        src_out[:, h * LOW : (h + 1) * LOW] = piece[:5]
        pieces.extend(split(piece))
    picked = lax.dot_general(
        jnp.concatenate(pieces, axis=0).astype(BF16),
        low_hot[...],
        NN,
        preferred_element_type=F32,
    )
    total = jnp.zeros((8, blocks), F32)
    for h in range(high):
        piece = picked[16 * h : 16 * h + 8] + picked[16 * h + 8 : 16 * h + 16]
        total = jnp.where(source_high == h, piece, total)
    chosen[...] = total

    def residual_sums(g, carry):
        rows = pl.ds(pl.multiple_of(g * LANES, LANES), LANES)
        x = [jnp.broadcast_to(chosen[c : c + 1, rows], (8, LANES)) for c in range(5)]
        totals = None
        for t in range(LANES // 8):
            tile = pl.ds(t * 8, 8)
            taken = src_t[g, 0, tile, :] * x[0]
            for c in range(1, 5):
                taken = taken + src_t[g, c, tile, :] * x[c]
            residual = src_t[g, 5, tile, :] - taken
            b = [basis_t[g, j, tile, :] for j in range(4)]
            h = [att_t[g, c, tile, :] * residual for c in range(4)]
            terms = [b[j] * h[c] for j in range(4) for c in range(4)]
            terms.append(cal_t[g, tile, :] * residual)
            totals = terms if totals is None else [x_ + y_ for x_, y_ in zip(totals, terms)]
        for j in range(4):
            for c in range(4):
                q = j * 8 + c
                knot_sums[q : q + 1, rows] = fold(totals[j * 4 + c])
        unit_sums[0:1, rows] = fold(totals[16])
        return carry

    lax.fori_loop(0, groups, residual_sums, 0)

    unit_pair = jnp.where(live, unit_sums[0:2, :], 0.0)
    first, second = split(unit_pair)
    local_high = (local >> 7).astype(F32)
    local_low = (local & (LANES - 1)).astype(F32)
    fields = jnp.concatenate(
        [first, local_high, local_low, second, jnp.zeros((2, blocks), F32)], axis=0
    )
    for o in range(0, devices, 2):
        both = [jnp.where(owner == o + i, fields, 0.0) for i in range(2)]
        spread[8 * o : 8 * o + 16, :] = jnp.concatenate(both, axis=0).astype(BF16)
    packed = lax.dot_general(
        spread[: 8 * devices, :], slot_hot[...], NT, preferred_element_type=F32
    )
    for o in range(devices):
        unit_send[o] = packed[8 * o : 8 * o + 4] + packed[8 * o + 4 : 8 * o + 8]

    unit_copies = []
    for k in range(1, devices):
        copy = pltpu.make_async_remote_copy(
            src_ref=unit_send.at[lax.rem(me + k, devices)],
            dst_ref=unit_in.at[k],
            send_sem=unit_sems.at[0, k],
            recv_sem=unit_sems.at[1, k],
            device_id=any_peer(k),
            device_id_type=MESH,
        )
        copy.start()
        unit_copies.append(copy)

    segment = segment_ref[...]
    segment_high = segment >> 7
    segment_hot = one_hot(SEG_DEV, segment & (SEG_DEV - 1))
    pair = jnp.concatenate(split(jnp.where(live, knot_sums[...], 0.0)), axis=0)
    for h in range(n_sky):
        spread[64 * h : 64 * h + 64, :] = jnp.where(segment_high == h, pair, 0.0).astype(BF16)
    placed = lax.dot_general(
        spread[: 64 * n_sky, :], segment_hot, NT, preferred_element_type=F32
    )
    wide = jnp.concatenate(
        [placed[64 * h : 64 * h + 32] + placed[64 * h + 32 : 64 * h + 64] for h in range(n_sky)],
        axis=1,
    )
    knots = wide[0:8]
    position = lax.broadcasted_iota(jnp.int32, knots.shape, 1)
    for j in range(1, 4):
        moved = pltpu.roll(wide[8 * j : 8 * j + 8], j, 1)
        knots = knots + jnp.where(position >= j, moved, 0.0)
    for h in range(n_sky):
        knot_send[h] = knots[:, h * SEG_DEV : (h + 1) * SEG_DEV]

    knot_copies = []
    for k in range(1, plane):
        q = lax.rem(plane_me + k, plane)
        peer_sky = lax.div(q, n_fov)
        copy = pltpu.make_async_remote_copy(
            src_ref=knot_send.at[peer_sky],
            dst_ref=knot_in.at[k],
            send_sem=knot_sems.at[0, k],
            recv_sem=knot_sems.at[1, k],
            device_id=(peer_sky, tm, lax.rem(q, n_fov)),
            device_id_type=MESH,
        )
        copy.start()
        knot_copies.append(copy)

    for copy in unit_copies:
        copy.wait_recv()
    unit_in[0] = unit_send[me]
    flat = jnp.concatenate([unit_in[k] for k in range(devices)], axis=1)
    first, second = split(flat[0:2])
    flat_high = flat[2:3].astype(jnp.int32)
    flat_low = flat[3:4].astype(jnp.int32)
    high_hit = (
        lax.broadcasted_iota(jnp.int32, (unit_high, flat.shape[1]), 0) == flat_high
    )
    rows = [first[0:1], second[0:1], first[1:2], second[1:2]]
    spread_units = jnp.concatenate(
        [jnp.where(high_hit, value, 0.0).astype(BF16) for value in rows], axis=0
    )
    units = lax.dot_general(
        spread_units, one_hot(LANES, flat_low), NT, preferred_element_type=F32
    )
    n = unit_high
    cal_out[...] = (units[:n] + units[n : 2 * n]) / (
        1.0 + (units[2 * n : 3 * n] + units[3 * n :])
    )

    for copy in knot_copies:
        copy.wait_recv()
    total = knot_send[sky]
    for k in range(1, plane):
        total = total + knot_in[k]
    att_out[...] = total[0:4] / (1.0 + total[4:8])

    for copy in table_copies + update_copies + unit_copies + knot_copies:
        copy.wait_send()


def shards(sizes, src, att, cal, phase, res, source, segment, unit, live):
    n_sky, n_tm, n_fov = sizes
    devices = n_sky * n_tm * n_fov
    blocks = src.shape[0]
    groups = blocks // LANES
    parts = n_tm * n_fov
    plane = n_sky * n_fov
    high = SRC_DEV // LOW
    per_part = high // parts
    spread_rows = max(48 * high, 8 * devices, 64 * n_sky)
    anywhere = pl.BlockSpec(memory_space=pl.ANY)
    vmem = pl.BlockSpec(memory_space=pltpu.VMEM)
    smem = pl.BlockSpec(memory_space=pltpu.SMEM)
    dma = pltpu.SemaphoreType.DMA
    src_update, att_update, cal_update = pl.pallas_call(
        functools.partial(kernel, sizes),
        out_shape=(
            jax.ShapeDtypeStruct((5, SRC_DEV), F32),
            jax.ShapeDtypeStruct((4, SEG_DEV), F32),
            jax.ShapeDtypeStruct((CAL // devices // LANES, LANES), F32),
        ),
        in_specs=[anywhere] * 5 + [vmem] * 3 + [smem],
        out_specs=(vmem, vmem, vmem),
        scratch_shapes=[
            pltpu.VMEM((src.shape[1], blocks, LANES), F32),
            pltpu.VMEM(att.shape, F32),
            pltpu.VMEM(cal.shape, F32),
            pltpu.VMEM(phase.shape, F32),
            pltpu.VMEM(res.shape, F32),
            pltpu.VMEM((groups, 6, LANES, LANES), F32),
            pltpu.VMEM((groups, 4, LANES, LANES), F32),
            pltpu.VMEM((groups, 4, LANES, LANES), F32),
            pltpu.VMEM((groups, LANES, LANES), F32),
            pltpu.VMEM((24, blocks), F32),
            pltpu.VMEM((32, blocks), F32),
            pltpu.VMEM((8, blocks), F32),
            pltpu.VMEM((LOW, blocks), BF16),
            pltpu.VMEM((spread_rows, blocks), BF16),
            pltpu.VMEM((parts, per_part, 24, LOW), F32),
            pltpu.VMEM((parts, per_part, 24, LOW), F32),
            pltpu.VMEM((parts, per_part, 8, LOW), F32),
            pltpu.VMEM((8, blocks), F32),
            pltpu.VMEM((1, blocks), F32),
            pltpu.VMEM((LANES, blocks), BF16),
            pltpu.VMEM((n_sky, 8, SEG_DEV), F32),
            pltpu.VMEM((plane, 8, SEG_DEV), F32),
            pltpu.VMEM((devices, 4, LANES), F32),
            pltpu.VMEM((devices, 4, LANES), F32),
            dma((2, groups)),
            dma((3,)),
            dma((2, parts)),
            dma((2, parts)),
            dma((2, plane)),
            dma((2, devices)),
        ],
        compiler_params=pltpu.CompilerParams(
            collective_id=0, has_side_effects=True, vmem_limit_bytes=58 * 1024 * 1024
        ),
    )(
        jnp.transpose(src, (1, 0, 2)),
        att,
        cal,
        phase,
        res,
        source.reshape(1, blocks),
        segment.reshape(1, blocks),
        unit.reshape(1, blocks),
        live,
    )
    return (
        src_update,
        att_update.reshape(4, 1, SEG_DEV),
        cal_update.reshape(CAL // devices),
    )


def solution(mesh):
    sizes = (mesh.shape["sky"], mesh.shape["tm"], mesh.shape["fov"])
    every = ("sky", "tm", "fov")
    return jax.shard_map(
        functools.partial(shards, sizes),
        mesh=mesh,
        in_specs=(
            P(every, None, None),
            P(every, None, None),
            P(every, None),
            P(every, None),
            P(every, None),
            P(every),
            P(every),
            P(every),
            P(every),
        ),
        out_specs=(P(None, "sky"), P(None, "tm", "sky"), P(every)),
        check_vma=False,
    )
```

time: 398 us -> 43.2 us (0.11); the launches traced: 393 us -> 42.9 us
  waiting for transfers between devices: 178 us -> 0 us
  other arithmetic: 129 us -> 0 us
  matrix products: 38 us -> 0 us
  Pallas kernels: 0 us -> 37.4 us
  local copies, waits for them, and re-layouts: 28.5 us -> 4.27 us
  between operations: 15 us -> 1.29 us
  blocking collectives: 4.19 us -> 0 us
    psum x2 -> x0, waiting for transfers between devices: 174 us -> none  [the longest x1 143 us: shards(): lax.psum((unit_right, unit_diag), ('sky', 'tm', 'fov'))]
    scatter-add x5 -> x0, other arithmetic: 94.6 us -> none  [the longest x1 44.4 us: shards(): jax.ops.segment_sum(values.reshape(-1, 8), knot_index.reshape(-1), num_se...]
    dot_general x2 -> x0, matrix products: 38 us -> none  [the longest x1 19.9 us: spline_products(): jnp.einsum('bjo,bco->bjc', basis, weighted, precision=lax.Precision.HIGHEST)]
    pallas_call x0 -> x1, Pallas kernels: none -> 37.4 us  [shards(): pl.pallas_call(functools.partial(kernel, sizes), out_shape=(jax.ShapeDtyp...]
    reduce_sum x4 -> x0, other arithmetic: 24.8 us -> none  [the longest x1 13.6 us: shards(): residual = obs_residual - jnp.sum(src_partials * chosen[:, :, None], axis=1)]
    div x5 -> x0, other arithmetic: 9.31 us -> none  [the longest x1 2.38 us: solve_normals(): forward.append(running / factor[i, i])]
    gather x2 -> x0, local copies, waits for them, and re-layouts: 9.22 us -> none  [shards(): chosen = src_update[:, block_source].T]
    mul x5 -> x0, local copies, waits for them, and re-layouts: 6.28 us -> none  [the longest x3 3.56 us: shards(): spline_products(residual, att_partials, obs_phase)]
  transfers between devices with their start and end apart: 3 -> 0, of which waited for: 3 -> 0; matrix products, arithmetic and copies ran while one was open for 13% -> 0% of each run, Pallas kernels for 0% -> 0%
where the time goes in v1:
time: 43.2 us; the launch traced here: 42.9 us
  Pallas kernels  37.4 us (87%)
  local copies, waits for them, and re-layouts  4.27 us (10%)
  between operations  1.29 us (3%)
    pallas_call x1, Pallas kernels, shards(): pl.pallas_call(functools.partial(kernel, sizes), out_shape=(jax.ShapeDtyp...  37.4 us
    unnamed x3, local copies, waits for them, and re-layouts  4.27 us

profile of v1, /device:TPU:0, one launch (start us, length us, event | category | flops | bytes accessed | tf_op | source)
XLA Modules:
  0.0 42.9 jit_solution(8283251938599035591)
XLA Ops:
  1.3 37.4 %shard_map.112 = (f32[5,4096]{1,0:T(8,128)}, f32[4,128]{1,0:T(4,128)}, f32[128,128]{1,0:T(8,128)}) custom-call(f32[5,2048,128]{2,1,0:T(8,128)} %bitcast.8, f32[2048,4,128]{2,1,0:T(4,128)} %att_hbm.1, f32[2048,128]{1,0:T(8,128)} %cal_hbm.1, f32[2048,128]{1,0:T(8,128)} %phase_hbm.1, f32[2048,128]{1,0:T(8,128)} %res_hbm.1, s32[1,2048]{1,0:T(1,128)} %bitcast.10, ...), custom_call_target="tpu_custom_call" | custom-call | tf_op jit(solution)/shard_map/pallas_call | solution.py:457
  38.7 1.6 %copy.17 = f32[5,4096]{1,0:T(8,128)} copy(f32[5,4096]{1,0:T(8,128)} %get-tuple-element.15) | data formatting | bytes 163840
  40.2 1.2 %copy.18 = f32[4,1,128]{2,1,0:T(1,128)} copy(f32[4,1,128]{2,1,0:T(1,128)} %bitcast.13) | data formatting | bytes 4096
  41.5 1.5 %copy.19 = f32[16384]{0:T(1024)} copy(f32[16384]{0:T(1024)} %bitcast.9) | data formatting | bytes 131072

commit v2 on v1

--- a/solution.py
+++ b/solution.py
@@ -79,8 +79,8 @@
     unit_ref,
     live_ref,
     src_out,
-    att_out,
-    cal_out,
+    knot_out,
+    unit_out,
     src_in,
     att_in,
     cal_in,
@@ -96,7 +96,10 @@
     low_hot,
     spread,
     table,
+    fov_in,
+    half,
     table_in,
+    total_ref,
     update,
     chosen,
     rank_row,
@@ -107,6 +110,7 @@
     unit_in,
     chunk_sems,
     whole_sems,
+    fov_sems,
     table_sems,
     update_sems,
     knot_sems,
@@ -121,13 +125,13 @@
     per_part = high // parts
     plane = n_sky * n_fov
     share = CAL // devices
-    unit_high = share // LANES
+    cuts = SRC_DEV // parts // LANES
 
     sky = lax.axis_index("sky")
     tm = lax.axis_index("tm")
     fov = lax.axis_index("fov")
     me = (sky * n_tm + tm) * n_fov + fov
-    part_me = tm * n_fov + fov
+    part_me = fov * n_tm + tm
     plane_me = sky * n_fov + fov
 
     def any_peer(k):
@@ -138,10 +142,6 @@
             lax.rem(q, n_fov),
         )
 
-    barrier = pltpu.get_barrier_semaphore()
-    for k in range(1, devices):
-        pl.semaphore_signal(barrier, inc=1, device_id=any_peer(k), device_id_type=MESH)
-
     def chunk_copies(g):
         rows = pl.ds(pl.multiple_of(g * LANES, LANES), LANES)
         return (
@@ -163,6 +163,14 @@
     lax.fori_loop(0, groups, start_chunk, 0)
     for copy in whole_copies:
         copy.start()
+
+    barrier = pltpu.get_barrier_semaphore()
+    for k in range(1, devices):
+        pl.semaphore_signal(barrier, inc=1, device_id=any_peer(k), device_id_type=MESH)
+
+    source = source_ref[...]
+    source_high = source >> 8
+    low_hot[...] = one_hot(LOW, source & (LOW - 1))
 
     def source_sums(g, carry):
         for copy in chunk_copies(g):
@@ -185,9 +193,6 @@
     sums[20:24, :] = jnp.zeros((4, blocks), F32)
 
     live = lax.broadcasted_iota(jnp.int32, (1, blocks), 1) < live_ref[0]
-    source = source_ref[...]
-    source_high = source >> 8
-    low_hot[...] = one_hot(LOW, source & (LOW - 1))
     pair = jnp.concatenate(split(jnp.where(live, sums[...], 0.0)), axis=0)
     for h in range(high):
         spread[48 * h : 48 * h + 48, :] = jnp.where(source_high == h, pair, 0.0).astype(BF16)
@@ -195,25 +200,29 @@
         spread[: 48 * high, :], low_hot[...], NT, preferred_element_type=F32
     )
     for h in range(high):
-        table[h // per_part, h % per_part] = (
-            placed[48 * h : 48 * h + 24] + placed[48 * h + 24 : 48 * h + 48]
-        )
+        piece = placed[48 * h : 48 * h + 24] + placed[48 * h + 24 : 48 * h + 48]
+        p = h // per_part
+        for l in range(LOW // LANES):
+            row = ((h % per_part) * (LOW // LANES) + l) * 20
+            table[p // n_tm, p % n_tm, row : row + 20, :] = piece[
+                :20, l * LANES : (l + 1) * LANES
+            ]
 
     pl.semaphore_wait(barrier, devices - 1)
 
-    table_copies = []
-    for k in range(1, parts):
-        p = lax.rem(part_me + k, parts)
+    fov_copies = []
+    for k in range(1, n_fov):
+        f = lax.rem(fov + k, n_fov)
         copy = pltpu.make_async_remote_copy(
-            src_ref=table.at[p],
-            dst_ref=table_in.at[k],
-            send_sem=table_sems.at[0, k],
-            recv_sem=table_sems.at[1, k],
-            device_id=(sky, lax.div(p, n_fov), lax.rem(p, n_fov)),
+            src_ref=table.at[f],
+            dst_ref=fov_in.at[k],
+            send_sem=fov_sems.at[0, k],
+            recv_sem=fov_sems.at[1, k],
+            device_id=(sky, tm, f),
             device_id_type=MESH,
         )
         copy.start()
-        table_copies.append(copy)
+        fov_copies.append(copy)
 
     for copy in whole_copies:
         copy.wait()
@@ -248,7 +257,54 @@
         unit_sums[1:2, rows] = fold(totals[16])
         return carry
 
-    lax.fori_loop(0, groups, fixed_sums, 0)
+    lax.fori_loop(0, groups // 4, fixed_sums, 0)
+
+    for copy in fov_copies:
+        copy.wait_recv()
+    for t in range(n_tm):
+        total = table[fov, t]
+        for k in range(1, n_fov):
+            total = total + fov_in[k, t]
+        half[t] = total
+    table_copies = []
+    for k in range(1, n_tm):
+        t = lax.rem(tm + k, n_tm)
+        copy = pltpu.make_async_remote_copy(
+            src_ref=half.at[t],
+            dst_ref=table_in.at[k],
+            send_sem=table_sems.at[0, k],
+            recv_sem=table_sems.at[1, k],
+            device_id=(sky, t, fov),
+            device_id_type=MESH,
+        )
+        copy.start()
+        table_copies.append(copy)
+
+    lax.fori_loop(groups // 4, groups, fixed_sums, 0)
+
+    for copy in table_copies:
+        copy.wait_recv()
+    total = half[tm]
+    for k in range(1, n_tm):
+        total = total + table_in[k]
+    total_ref[...] = total
+    solved = solve_rows([total_ref[pl.ds(q, cuts, stride=20), :] for q in range(20)])
+    for c in range(5):
+        update[part_me, c * cuts : (c + 1) * cuts, :] = solved[c]
+
+    update_copies = []
+    for k in range(1, parts):
+        p = lax.rem(part_me + k, parts)
+        copy = pltpu.make_async_remote_copy(
+            src_ref=update.at[part_me],
+            dst_ref=update.at[part_me],
+            send_sem=update_sems.at[0, k],
+            recv_sem=update_sems.at[1, k],
+            device_id=(sky, lax.rem(p, n_tm), lax.div(p, n_tm)),
+            device_id_type=MESH,
+        )
+        copy.start()
+        update_copies.append(copy)
 
     unit = unit_ref[...]
     owner = lax.div(unit, share)
@@ -266,30 +322,6 @@
         before = before + counts[:, LANES:]
     slot_hot[...] = one_hot(LANES, rank_row[...].astype(jnp.int32))
 
-    for copy in table_copies:
-        copy.wait_recv()
-    for s in range(per_part):
-        total = table[part_me, s]
-        for k in range(1, parts):
-            total = total + table_in[k, s]
-        solved = solve_rows([total[q : q + 1] for q in range(20)])
-        for c in range(5):
-            update[part_me, s, c : c + 1, :] = solved[c]
-        update[part_me, s, 5:8, :] = jnp.zeros((3, LOW), F32)
-
-    update_copies = []
-    for k in range(1, parts):
-        p = lax.rem(part_me + k, parts)
-        copy = pltpu.make_async_remote_copy(
-            src_ref=update.at[part_me],
-            dst_ref=update.at[part_me],
-            send_sem=update_sems.at[0, k],
-            recv_sem=update_sems.at[1, k],
-            device_id=(sky, lax.div(p, n_fov), lax.rem(p, n_fov)),
-            device_id_type=MESH,
-        )
-        copy.start()
-        update_copies.append(copy)
     for k in range(1, parts):
         p = lax.rem(part_me + parts - k, parts)
         pltpu.make_async_remote_copy(
@@ -297,15 +329,22 @@
             dst_ref=update.at[p],
             send_sem=update_sems.at[0, k],
             recv_sem=update_sems.at[1, k],
-            device_id=(sky, lax.div(p, n_fov), lax.rem(p, n_fov)),
+            device_id=(sky, lax.rem(p, n_tm), lax.div(p, n_tm)),
             device_id_type=MESH,
         ).wait_recv()
 
     pieces = []
     for h in range(high):
-        piece = update[h // per_part, h % per_part]
-        src_out[:, h * LOW : (h + 1) * LOW] = piece[:5]
-        pieces.extend(split(piece))
+        start = (h % per_part) * (LOW // LANES)
+        piece = jnp.concatenate(
+            [
+                update[h // per_part, pl.ds(start + l, 5, stride=cuts), :]
+                for l in range(LOW // LANES)
+            ],
+            axis=1,
+        )
+        src_out[:, h * LOW : (h + 1) * LOW] = piece
+        pieces.extend(split(jnp.concatenate([piece, jnp.zeros((3, LOW), F32)], axis=0)))
     picked = lax.dot_general(
         jnp.concatenate(pieces, axis=0).astype(BF16),
         low_hot[...],
@@ -410,34 +449,37 @@
     for copy in unit_copies:
         copy.wait_recv()
     unit_in[0] = unit_send[me]
-    flat = jnp.concatenate([unit_in[k] for k in range(devices)], axis=1)
-    first, second = split(flat[0:2])
-    flat_high = flat[2:3].astype(jnp.int32)
-    flat_low = flat[3:4].astype(jnp.int32)
-    high_hit = (
-        lax.broadcasted_iota(jnp.int32, (unit_high, flat.shape[1]), 0) == flat_high
-    )
-    rows = [first[0:1], second[0:1], first[1:2], second[1:2]]
-    spread_units = jnp.concatenate(
-        [jnp.where(high_hit, value, 0.0).astype(BF16) for value in rows], axis=0
-    )
-    units = lax.dot_general(
-        spread_units, one_hot(LANES, flat_low), NT, preferred_element_type=F32
-    )
-    n = unit_high
-    cal_out[...] = (units[:n] + units[n : 2 * n]) / (
-        1.0 + (units[2 * n : 3 * n] + units[3 * n :])
-    )
+    unit_out[...] = jnp.concatenate([unit_in[k] for k in range(devices)], axis=1)
 
     for copy in knot_copies:
         copy.wait_recv()
     total = knot_send[sky]
     for k in range(1, plane):
         total = total + knot_in[k]
-    att_out[...] = total[0:4] / (1.0 + total[4:8])
-
-    for copy in table_copies + update_copies + unit_copies + knot_copies:
+    knot_out[...] = total
+
+    for copy in fov_copies + table_copies + update_copies + unit_copies + knot_copies:
         copy.wait_send()
+
+
+def finish(src_ref, knot_ref, unit_ref, src_out, att_out, cal_out):
+    src_out[...] = src_ref[...]
+    att_out[...] = knot_ref[0:4] / (1.0 + knot_ref[4:8])
+    n = cal_out.shape[0]
+    first, second = split(unit_ref[0:2])
+    flat_high = unit_ref[2:3].astype(jnp.int32)
+    flat_low = unit_ref[3:4].astype(jnp.int32)
+    high_hit = lax.broadcasted_iota(jnp.int32, (n, unit_ref.shape[1]), 0) == flat_high
+    rows = [first[0:1], second[0:1], first[1:2], second[1:2]]
+    spread_units = jnp.concatenate(
+        [jnp.where(high_hit, value, 0.0).astype(BF16) for value in rows], axis=0
+    )
+    units = lax.dot_general(
+        spread_units, one_hot(LANES, flat_low), NT, preferred_element_type=F32
+    )
+    cal_out[...] = (units[:n] + units[n : 2 * n]) / (
+        1.0 + (units[2 * n : 3 * n] + units[3 * n :])
+    )
 
 
 def shards(sizes, src, att, cal, phase, res, source, segment, unit, live):
@@ -448,18 +490,18 @@
     parts = n_tm * n_fov
     plane = n_sky * n_fov
     high = SRC_DEV // LOW
-    per_part = high // parts
+    cuts = SRC_DEV // parts // LANES
     spread_rows = max(48 * high, 8 * devices, 64 * n_sky)
     anywhere = pl.BlockSpec(memory_space=pl.ANY)
     vmem = pl.BlockSpec(memory_space=pltpu.VMEM)
     smem = pl.BlockSpec(memory_space=pltpu.SMEM)
     dma = pltpu.SemaphoreType.DMA
-    src_update, att_update, cal_update = pl.pallas_call(
+    updates, knots, units = pl.pallas_call(
         functools.partial(kernel, sizes),
         out_shape=(
             jax.ShapeDtypeStruct((5, SRC_DEV), F32),
-            jax.ShapeDtypeStruct((4, SEG_DEV), F32),
-            jax.ShapeDtypeStruct((CAL // devices // LANES, LANES), F32),
+            jax.ShapeDtypeStruct((8, SEG_DEV), F32),
+            jax.ShapeDtypeStruct((4, devices * LANES), F32),
         ),
         in_specs=[anywhere] * 5 + [vmem] * 3 + [smem],
         out_specs=(vmem, vmem, vmem),
@@ -478,9 +520,12 @@
             pltpu.VMEM((8, blocks), F32),
             pltpu.VMEM((LOW, blocks), BF16),
             pltpu.VMEM((spread_rows, blocks), BF16),
-            pltpu.VMEM((parts, per_part, 24, LOW), F32),
-            pltpu.VMEM((parts, per_part, 24, LOW), F32),
-            pltpu.VMEM((parts, per_part, 8, LOW), F32),
+            pltpu.VMEM((n_fov, n_tm, 20 * cuts, LANES), F32),
+            pltpu.VMEM((n_fov, n_tm, 20 * cuts, LANES), F32),
+            pltpu.VMEM((n_tm, 20 * cuts, LANES), F32),
+            pltpu.VMEM((n_tm, 20 * cuts, LANES), F32),
+            pltpu.VMEM((20 * cuts, LANES), F32),
+            pltpu.VMEM((parts, 5 * cuts, LANES), F32),
             pltpu.VMEM((8, blocks), F32),
             pltpu.VMEM((1, blocks), F32),
             pltpu.VMEM((LANES, blocks), BF16),
@@ -490,7 +535,8 @@
             pltpu.VMEM((devices, 4, LANES), F32),
             dma((2, groups)),
             dma((3,)),
-            dma((2, parts)),
+            dma((2, n_fov)),
+            dma((2, n_tm)),
             dma((2, parts)),
             dma((2, plane)),
             dma((2, devices)),
@@ -509,6 +555,17 @@
         unit.reshape(1, blocks),
         live,
     )
+    src_update, att_update, cal_update = pl.pallas_call(
+        finish,
+        out_shape=(
+            jax.ShapeDtypeStruct((5, SRC_DEV), F32),
+            jax.ShapeDtypeStruct((4, SEG_DEV), F32),
+            jax.ShapeDtypeStruct((CAL // devices // LANES, LANES), F32),
+        ),
+        in_specs=[vmem] * 3,
+        out_specs=(vmem, vmem, vmem),
+        compiler_params=pltpu.CompilerParams(vmem_limit_bytes=40 * 1024 * 1024),
+    )(updates, knots, units)
     return (
         src_update,
         att_update.reshape(4, 1, SEG_DEV),

time: 43.2 us -> 36.6 us (0.85)
  Pallas kernels: 37.4 us -> 32.6 us
  local copies, waits for them, and re-layouts: 4.27 us -> 2.42 us
    pallas_call x1, Pallas kernels: 37.4 us -> 30.7 us  [shards(): pl.pallas_call(functools.partial(kernel, sizes), out_shape=(jax.ShapeDtyp...]
    pallas_call x0 -> x1, Pallas kernels: none -> 1.92 us  [shards(): pl.pallas_call(finish, out_shape=(jax.ShapeDtypeStruct((5, SRC_DEV), F32)...]
    unnamed x3 -> x6, local copies, waits for them, and re-layouts: 4.27 us -> 2.42 us
where the time goes in v2:
time: 36.6 us; the launch traced here: 36.3 us
  Pallas kernels  32.6 us (89%)
  local copies, waits for them, and re-layouts  2.42 us (7%)
  between operations  1.3 us (4%)
    pallas_call x1, Pallas kernels, shards(): pl.pallas_call(functools.partial(kernel, sizes), out_shape=(jax.ShapeDtyp...  30.7 us
    unnamed x6, local copies, waits for them, and re-layouts  2.42 us
    pallas_call x1, Pallas kernels, shards(): pl.pallas_call(finish, out_shape=(jax.ShapeDtypeStruct((5, SRC_DEV), F32)...  1.92 us

profile of v2, /device:TPU:0, one launch (start us, length us, event | category | flops | bytes accessed | tf_op | source)
XLA Modules:
  0.0 36.3 jit_solution(16838348165299774309)
XLA Ops:
  1.3 30.7 %shard_map.112 = (f32[5,4096]{1,0:T(8,128)}, f32[8,128]{1,0:T(8,128)}, f32[4,4096]{1,0:T(4,128)}) custom-call(f32[5,2048,128]{2,1,0:T(8,128)} %bitcast.8, f32[2048,4,128]{2,1,0:T(4,128)} %att_hbm.1, f32[2048,128]{1,0:T(8,128)} %cal_hbm.1, f32[2048,128]{1,0:T(8,128)} %phase_hbm.1, f32[2048,128]{1,0:T(8,128)} %res_hbm.1, s32[1,2048]{1,0:T(1,128)} %bitcast.9, ...), custom_call_target="tpu_custom_call" | custom-call | tf_op jit(solution)/shard_map/pallas_call | solution.py:499
  32.0 0.0 copy-start
  32.0 0.9 %copy-done = f32[5,4096]{1,0:T(8,128)S(1)} copy-done((f32[5,4096]{1,0:T(8,128)S(1)}, f32[5,4096]{1,0:T(8,128)}, u32[]{:S(2)}) %copy-start) | copy-done | bytes 81944
  32.9 0.0 copy-start.1
  32.9 0.8 %copy-done.1 = f32[4,4096]{1,0:T(4,128)S(1)} copy-done((f32[4,4096]{1,0:T(4,128)S(1)}, f32[4,4096]{1,0:T(4,128)}, u32[]{:S(2)}) %copy-start.1) | copy-done | bytes 65560
  33.7 0.0 copy-start.2
  33.7 0.7 %copy-done.2 = f32[8,128]{1,0:T(8,128)S(1)} copy-done((f32[8,128]{1,0:T(8,128)S(1)}, f32[8,128]{1,0:T(8,128)}, u32[]{:S(2)}) %copy-start.2) | copy-done | bytes 4120
  34.4 1.9 %shard_map.113 = (f32[5,4096]{1,0:T(8,128)}, f32[4,128]{1,0:T(4,128)}, f32[128,128]{1,0:T(8,128)}) custom-call(f32[5,4096]{1,0:T(8,128)S(1)} %copy-done, f32[8,128]{1,0:T(8,128)S(1)} %copy-done.2, f32[4,4096]{1,0:T(4,128)S(1)} %copy-done.1), custom_call_target="tpu_custom_call" | custom-call | tf_op jit(solution)/shard_map/pallas_call | solution.py:558
Async XLA Ops:
  32.0 0.9 %copy-start = (f32[5,4096]{1,0:T(8,128)S(1)}, f32[5,4096]{1,0:T(8,128)}, u32[]{:S(2)}) copy-start(f32[5,4096]{1,0:T(8,128)} %get-tuple-element.9.src_ref) | copy-start | bytes 245764
  32.9 0.8 %copy-start.1 = (f32[4,4096]{1,0:T(4,128)S(1)}, f32[4,4096]{1,0:T(4,128)}, u32[]{:S(2)}) copy-start(f32[4,4096]{1,0:T(4,128)} %get-tuple-element.11.unit_ref) | copy-start | bytes 196612
  33.7 0.7 %copy-start.2 = (f32[8,128]{1,0:T(8,128)S(1)}, f32[8,128]{1,0:T(8,128)}, u32[]{:S(2)}) copy-start(f32[8,128]{1,0:T(8,128)} %get-tuple-element.10.knot_ref) | copy-start | bytes 12292

commit v3 on v2

--- a/solution.py
+++ b/solution.py
@@ -15,6 +15,7 @@
 F32 = jnp.float32
 BF16 = jnp.bfloat16
 MESH = pl.DeviceIdType.MESH
+UNROLL = 4
 
 index_pairs = [(i, j) for i in range(5) for j in range(i, 5)]
 NT = (((1,), (1,)), ((), ()))
@@ -65,6 +66,16 @@
 
 def fold(total):
     return jnp.sum(total, axis=0, keepdims=True)
+
+
+def fold_all(scratch, totals):
+    count = len(totals)
+    for q, total in enumerate(totals):
+        scratch[q * 8 : q * 8 + 8, :] = total
+    folded = scratch[pl.ds(0, count, stride=8), :]
+    for s in range(1, 8):
+        folded = folded + scratch[pl.ds(s, count, stride=8), :]
+    return folded
 
 
 def kernel(
@@ -100,6 +111,10 @@
     half,
     table_in,
     total_ref,
+    folds_0,
+    folds_1,
+    folds_2,
+    folds_3,
     update,
     chosen,
     rank_row,
@@ -119,7 +134,8 @@
     n_sky, n_tm, n_fov = sizes
     devices = n_sky * n_tm * n_fov
     blocks = res_hbm.shape[0]
-    groups = blocks // LANES
+    steps = blocks // LANES // UNROLL
+    folds = (folds_0, folds_1, folds_2, folds_3)
     parts = n_tm * n_fov
     high = SRC_DEV // LOW
     per_part = high // parts
@@ -143,7 +159,8 @@
         )
 
     def chunk_copies(g):
-        rows = pl.ds(pl.multiple_of(g * LANES, LANES), LANES)
+        size = UNROLL * LANES
+        rows = pl.ds(pl.multiple_of(g * size, size), size)
         return (
             pltpu.make_async_copy(src_hbm.at[:, rows], src_in.at[:, rows], chunk_sems.at[0, g]),
             pltpu.make_async_copy(res_hbm.at[rows], res_in.at[rows], chunk_sems.at[1, g]),
@@ -160,7 +177,7 @@
             copy.start()
         return carry
 
-    lax.fori_loop(0, groups, start_chunk, 0)
+    lax.fori_loop(0, steps, start_chunk, 0)
     for copy in whole_copies:
         copy.start()
 
@@ -172,24 +189,27 @@
     source_high = source >> 8
     low_hot[...] = one_hot(LOW, source & (LOW - 1))
 
+    def group_rows(g, u):
+        return pl.ds(pl.multiple_of((g * UNROLL + u) * LANES, LANES), LANES)
+
     def source_sums(g, carry):
         for copy in chunk_copies(g):
             copy.wait()
-        rows = pl.ds(pl.multiple_of(g * LANES, LANES), LANES)
-        for c in range(5):
-            src_t[g, c] = src_in[c, rows, :].T
-        src_t[g, 5] = res_in[rows, :].T
-        totals = None
-        for t in range(LANES // 8):
-            tile = pl.ds(t * 8, 8)
-            a = [src_t[g, c, tile, :] for c in range(6)]
-            terms = [a[i] * a[j] for i, j in index_pairs] + [a[i] * a[5] for i in range(5)]
-            totals = terms if totals is None else [x + y for x, y in zip(totals, terms)]
-        for q in range(20):
-            sums[q : q + 1, rows] = fold(totals[q])
+        for u in range(UNROLL):
+            rows = group_rows(g, u)
+            for c in range(5):
+                src_t[g, u, c] = src_in[c, rows, :].T
+            src_t[g, u, 5] = res_in[rows, :].T
+            totals = None
+            for t in range(LANES // 8):
+                tile = pl.ds(t * 8, 8)
+                a = [src_t[g, u, c, tile, :] for c in range(6)]
+                terms = [a[i] * a[j] for i, j in index_pairs] + [a[i] * a[5] for i in range(5)]
+                totals = terms if totals is None else [x + y for x, y in zip(totals, terms)]
+            sums[0:20, rows] = fold_all(folds[u], totals)
         return carry
 
-    lax.fori_loop(0, groups, source_sums, 0)
+    lax.fori_loop(0, steps, source_sums, 0)
     sums[20:24, :] = jnp.zeros((4, blocks), F32)
 
     live = lax.broadcasted_iota(jnp.int32, (1, blocks), 1) < live_ref[0]
@@ -228,36 +248,35 @@
         copy.wait()
 
     def fixed_sums(g, carry):
-        rows = pl.ds(pl.multiple_of(g * LANES, LANES), LANES)
-        for c in range(4):
-            att_t[g, c] = att_in[rows, c, :].T
-        cal_t[g] = cal_in[rows, :].T
-        phase_t = phase_in[rows, :].T
-        rest = 1.0 - phase_t
-        square = phase_t * phase_t
-        cubed = square * phase_t
-        basis_t[g, 0] = rest * rest * rest * (1.0 / 6.0)
-        basis_t[g, 1] = (3.0 * cubed - 6.0 * square + 4.0) * (1.0 / 6.0)
-        basis_t[g, 2] = (-3.0 * cubed + 3.0 * square + 3.0 * phase_t + 1.0) * (1.0 / 6.0)
-        basis_t[g, 3] = cubed * (1.0 / 6.0)
-        totals = None
-        for t in range(LANES // 8):
-            tile = pl.ds(t * 8, 8)
-            b = [basis_t[g, j, tile, :] for j in range(4)]
-            h = [att_t[g, c, tile, :] for c in range(4)]
-            b = [x * x for x in b]
-            h = [x * x for x in h]
-            u = cal_t[g, tile, :]
-            terms = [b[j] * h[c] for j in range(4) for c in range(4)] + [u * u]
-            totals = terms if totals is None else [x + y for x, y in zip(totals, terms)]
-        for j in range(4):
+        for u in range(UNROLL):
+            rows = group_rows(g, u)
             for c in range(4):
-                q = j * 8 + 4 + c
-                knot_sums[q : q + 1, rows] = fold(totals[j * 4 + c])
-        unit_sums[1:2, rows] = fold(totals[16])
+                att_t[g, u, c] = att_in[rows, c, :].T
+            cal_t[g, u] = cal_in[rows, :].T
+            phase_t = phase_in[rows, :].T
+            rest = 1.0 - phase_t
+            square = phase_t * phase_t
+            cubed = square * phase_t
+            basis_t[g, u, 0] = rest * rest * rest * (1.0 / 6.0)
+            basis_t[g, u, 1] = (3.0 * cubed - 6.0 * square + 4.0) * (1.0 / 6.0)
+            basis_t[g, u, 2] = (-3.0 * cubed + 3.0 * square + 3.0 * phase_t + 1.0) * (1.0 / 6.0)
+            basis_t[g, u, 3] = cubed * (1.0 / 6.0)
+            totals = None
+            for t in range(LANES // 8):
+                tile = pl.ds(t * 8, 8)
+                b = [basis_t[g, u, j, tile, :] for j in range(4)]
+                h = [att_t[g, u, c, tile, :] for c in range(4)]
+                b = [x * x for x in b]
+                h = [x * x for x in h]
+                w = cal_t[g, u, tile, :]
+                terms = [b[j] * h[c] for j in range(4) for c in range(4)] + [w * w]
+                totals = terms if totals is None else [x + y for x, y in zip(totals, terms)]
+            folded = fold_all(folds[u], totals)
+            knot_sums[16:32, rows] = folded[0:16]
+            unit_sums[1:2, rows] = folded[16:17]
         return carry
 
-    lax.fori_loop(0, groups // 4, fixed_sums, 0)
+    lax.fori_loop(0, 1, fixed_sums, 0)
 
     for copy in fov_copies:
         copy.wait_recv()
@@ -280,7 +299,7 @@
         copy.start()
         table_copies.append(copy)
 
-    lax.fori_loop(groups // 4, groups, fixed_sums, 0)
+    lax.fori_loop(1, steps, fixed_sums, 0)
 
     for copy in table_copies:
         copy.wait_recv()
@@ -313,7 +332,7 @@
     column = lax.broadcasted_iota(jnp.int32, (LANES, 2 * LANES), 1)
     ramp = jnp.where(row <= column, 1.0, 0.0).astype(BF16)
     before = jnp.zeros((devices, LANES), F32)
-    for g in range(groups):
+    for g in range(blocks // LANES):
         cut = slice(g * LANES, (g + 1) * LANES)
         hot = lax.broadcasted_iota(jnp.int32, (devices, LANES), 0) == owner[:, cut]
         hot = jnp.where(hot, 1.0, 0.0)
@@ -358,28 +377,27 @@
     chosen[...] = total
 
     def residual_sums(g, carry):
-        rows = pl.ds(pl.multiple_of(g * LANES, LANES), LANES)
-        x = [jnp.broadcast_to(chosen[c : c + 1, rows], (8, LANES)) for c in range(5)]
-        totals = None
-        for t in range(LANES // 8):
-            tile = pl.ds(t * 8, 8)
-            taken = src_t[g, 0, tile, :] * x[0]
-            for c in range(1, 5):
-                taken = taken + src_t[g, c, tile, :] * x[c]
-            residual = src_t[g, 5, tile, :] - taken
-            b = [basis_t[g, j, tile, :] for j in range(4)]
-            h = [att_t[g, c, tile, :] * residual for c in range(4)]
-            terms = [b[j] * h[c] for j in range(4) for c in range(4)]
-            terms.append(cal_t[g, tile, :] * residual)
-            totals = terms if totals is None else [x_ + y_ for x_, y_ in zip(totals, terms)]
-        for j in range(4):
-            for c in range(4):
-                q = j * 8 + c
-                knot_sums[q : q + 1, rows] = fold(totals[j * 4 + c])
-        unit_sums[0:1, rows] = fold(totals[16])
+        for u in range(UNROLL):
+            rows = group_rows(g, u)
+            x = [jnp.broadcast_to(chosen[c : c + 1, rows], (8, LANES)) for c in range(5)]
+            totals = None
+            for t in range(LANES // 8):
+                tile = pl.ds(t * 8, 8)
+                taken = src_t[g, u, 0, tile, :] * x[0]
+                for c in range(1, 5):
+                    taken = taken + src_t[g, u, c, tile, :] * x[c]
+                residual = src_t[g, u, 5, tile, :] - taken
+                b = [basis_t[g, u, j, tile, :] for j in range(4)]
+                h = [att_t[g, u, c, tile, :] * residual for c in range(4)]
+                terms = [b[j] * h[c] for j in range(4) for c in range(4)]
+                terms.append(cal_t[g, u, tile, :] * residual)
+                totals = terms if totals is None else [y + z for y, z in zip(totals, terms)]
+            folded = fold_all(folds[u], totals)
+            knot_sums[0:16, rows] = folded[0:16]
+            unit_sums[0:1, rows] = folded[16:17]
         return carry
 
-    lax.fori_loop(0, groups, residual_sums, 0)
+    lax.fori_loop(0, steps, residual_sums, 0)
 
     unit_pair = jnp.where(live, unit_sums[0:2, :], 0.0)
     first, second = split(unit_pair)
@@ -423,11 +441,13 @@
         [placed[64 * h : 64 * h + 32] + placed[64 * h + 32 : 64 * h + 64] for h in range(n_sky)],
         axis=1,
     )
-    knots = wide[0:8]
-    position = lax.broadcasted_iota(jnp.int32, knots.shape, 1)
+    position = lax.broadcasted_iota(jnp.int32, (8, wide.shape[1]), 1)
+    knots = jnp.concatenate([wide[0:4], wide[16:20]], axis=0)
     for j in range(1, 4):
-        moved = pltpu.roll(wide[8 * j : 8 * j + 8], j, 1)
-        knots = knots + jnp.where(position >= j, moved, 0.0)
+        moved = jnp.concatenate(
+            [wide[4 * j : 4 * j + 4], wide[4 * j + 16 : 4 * j + 20]], axis=0
+        )
+        knots = knots + jnp.where(position >= j, pltpu.roll(moved, j, 1), 0.0)
     for h in range(n_sky):
         knot_send[h] = knots[:, h * SEG_DEV : (h + 1) * SEG_DEV]
 
@@ -462,8 +482,15 @@
         copy.wait_send()
 
 
-def finish(src_ref, knot_ref, unit_ref, src_out, att_out, cal_out):
-    src_out[...] = src_ref[...]
+def finish(src_hbm, knot_hbm, unit_hbm, src_out, att_out, cal_out, knot_ref, unit_ref, sems):
+    unit_copy = pltpu.make_async_copy(unit_hbm, unit_ref, sems.at[0])
+    knot_copy = pltpu.make_async_copy(knot_hbm, knot_ref, sems.at[1])
+    src_copy = pltpu.make_async_copy(src_hbm, src_out, sems.at[2])
+    unit_copy.start()
+    knot_copy.start()
+    src_copy.start()
+    unit_copy.wait()
+    knot_copy.wait()
     att_out[...] = knot_ref[0:4] / (1.0 + knot_ref[4:8])
     n = cal_out.shape[0]
     first, second = split(unit_ref[0:2])
@@ -480,13 +507,14 @@
     cal_out[...] = (units[:n] + units[n : 2 * n]) / (
         1.0 + (units[2 * n : 3 * n] + units[3 * n :])
     )
+    src_copy.wait()
 
 
 def shards(sizes, src, att, cal, phase, res, source, segment, unit, live):
     n_sky, n_tm, n_fov = sizes
     devices = n_sky * n_tm * n_fov
     blocks = src.shape[0]
-    groups = blocks // LANES
+    steps = blocks // LANES // UNROLL
     parts = n_tm * n_fov
     plane = n_sky * n_fov
     high = SRC_DEV // LOW
@@ -511,10 +539,10 @@
             pltpu.VMEM(cal.shape, F32),
             pltpu.VMEM(phase.shape, F32),
             pltpu.VMEM(res.shape, F32),
-            pltpu.VMEM((groups, 6, LANES, LANES), F32),
-            pltpu.VMEM((groups, 4, LANES, LANES), F32),
-            pltpu.VMEM((groups, 4, LANES, LANES), F32),
-            pltpu.VMEM((groups, LANES, LANES), F32),
+            pltpu.VMEM((steps, UNROLL, 6, LANES, LANES), F32),
+            pltpu.VMEM((steps, UNROLL, 4, LANES, LANES), F32),
+            pltpu.VMEM((steps, UNROLL, 4, LANES, LANES), F32),
+            pltpu.VMEM((steps, UNROLL, LANES, LANES), F32),
             pltpu.VMEM((24, blocks), F32),
             pltpu.VMEM((32, blocks), F32),
             pltpu.VMEM((8, blocks), F32),
@@ -525,6 +553,10 @@
             pltpu.VMEM((n_tm, 20 * cuts, LANES), F32),
             pltpu.VMEM((n_tm, 20 * cuts, LANES), F32),
             pltpu.VMEM((20 * cuts, LANES), F32),
+            pltpu.VMEM((160, LANES), F32),
+            pltpu.VMEM((160, LANES), F32),
+            pltpu.VMEM((160, LANES), F32),
+            pltpu.VMEM((160, LANES), F32),
             pltpu.VMEM((parts, 5 * cuts, LANES), F32),
             pltpu.VMEM((8, blocks), F32),
             pltpu.VMEM((1, blocks), F32),
@@ -533,7 +565,7 @@
             pltpu.VMEM((plane, 8, SEG_DEV), F32),
             pltpu.VMEM((devices, 4, LANES), F32),
             pltpu.VMEM((devices, 4, LANES), F32),
-            dma((2, groups)),
+            dma((2, steps)),
             dma((3,)),
             dma((2, n_fov)),
             dma((2, n_tm)),
@@ -562,9 +594,14 @@
             jax.ShapeDtypeStruct((4, SEG_DEV), F32),
             jax.ShapeDtypeStruct((CAL // devices // LANES, LANES), F32),
         ),
-        in_specs=[vmem] * 3,
-        out_specs=(vmem, vmem, vmem),
-        compiler_params=pltpu.CompilerParams(vmem_limit_bytes=40 * 1024 * 1024),
+        in_specs=[anywhere] * 3,
+        out_specs=(anywhere, vmem, vmem),
+        scratch_shapes=[
+            pltpu.VMEM(knots.shape, F32),
+            pltpu.VMEM(units.shape, F32),
+            dma((3,)),
+        ],
+        compiler_params=pltpu.CompilerParams(vmem_limit_bytes=58 * 1024 * 1024),
     )(updates, knots, units)
     return (
         src_update,

time: 36.6 us -> 36.7 us (level)
  Pallas kernels: 32.6 us -> 35.1 us
  local copies, waits for them, and re-layouts: 2.42 us -> 0 us
    pallas_call x1, Pallas kernels: 1.92 us -> 5.73 us  [shards(): pl.pallas_call(finish, out_shape=(jax.ShapeDtypeStruct((5, SRC_DEV), F32)...]
    unnamed x6 -> x0, local copies, waits for them, and re-layouts: 2.42 us -> none
    pallas_call x1, Pallas kernels: 30.7 us -> 29.4 us  [shards(): pl.pallas_call(functools.partial(kernel, sizes), out_shape=(jax.ShapeDtyp...]
where the time goes in v3:
time: 36.7 us; the launch traced here: 36.4 us
  Pallas kernels  35.1 us (96%)
  between operations  1.29 us (4%)
    pallas_call x1, Pallas kernels, shards(): pl.pallas_call(functools.partial(kernel, sizes), out_shape=(jax.ShapeDtyp...  29.4 us
    pallas_call x1, Pallas kernels, shards(): pl.pallas_call(finish, out_shape=(jax.ShapeDtypeStruct((5, SRC_DEV), F32)...  5.73 us

profile of v3, /device:TPU:0, one launch (start us, length us, event | category | flops | bytes accessed | tf_op | source)
XLA Modules:
  0.0 36.4 jit_solution(16750290520858756361)
XLA Ops:
  1.3 29.4 %shard_map.112 = (f32[5,4096]{1,0:T(8,128)}, f32[8,128]{1,0:T(8,128)}, f32[4,4096]{1,0:T(4,128)}) custom-call(f32[5,2048,128]{2,1,0:T(8,128)} %bitcast.8, f32[2048,4,128]{2,1,0:T(4,128)} %att_hbm.1, f32[2048,128]{1,0:T(8,128)} %cal_hbm.1, f32[2048,128]{1,0:T(8,128)} %phase_hbm.1, f32[2048,128]{1,0:T(8,128)} %res_hbm.1, s32[1,2048]{1,0:T(1,128)} %bitcast.9, ...), custom_call_target="tpu_custom_call" | custom-call | tf_op jit(solution)/shard_map/pallas_call | solution.py:527
  30.7 5.7 %shard_map.113 = (f32[5,4096]{1,0:T(8,128)}, f32[4,128]{1,0:T(4,128)}, f32[128,128]{1,0:T(8,128)}) custom-call(f32[5,4096]{1,0:T(8,128)} %get-tuple-element.9.src_hbm, f32[8,128]{1,0:T(8,128)} %get-tuple-element.10.knot_hbm, f32[4,4096]{1,0:T(4,128)} %get-tuple-element.11.unit_hbm), custom_call_target="tpu_custom_call" | custom-call | tf_op jit(solution)/shard_map/pallas_call | solution.py:590

commit v4 on v3

--- a/solution.py
+++ b/solution.py
@@ -90,8 +90,8 @@
     unit_ref,
     live_ref,
     src_out,
-    knot_out,
-    unit_out,
+    att_out,
+    cal_out,
     src_in,
     att_in,
     cal_in,
@@ -121,14 +121,18 @@
     slot_hot,
     knot_send,
     knot_in,
+    early_send,
+    early_in,
     unit_send,
     unit_in,
+    flat_hot,
     chunk_sems,
     whole_sems,
     fov_sems,
     table_sems,
     update_sems,
     knot_sems,
+    early_sems,
     unit_sems,
 ):
     n_sky, n_tm, n_fov = sizes
@@ -141,6 +145,7 @@
     per_part = high // parts
     plane = n_sky * n_fov
     share = CAL // devices
+    unit_high = share // LANES
     cuts = SRC_DEV // parts // LANES
 
     sky = lax.axis_index("sky")
@@ -341,6 +346,41 @@
         before = before + counts[:, LANES:]
     slot_hot[...] = one_hot(LANES, rank_row[...].astype(jnp.int32))
 
+    owned = lax.broadcasted_iota(jnp.int32, (devices, blocks), 0) == owner
+
+    def pack(rows):
+        for q, value in enumerate(rows):
+            spread[devices * q : devices * (q + 1), :] = jnp.where(owned, value, 0.0).astype(BF16)
+        packed = lax.dot_general(
+            spread[: devices * len(rows), :], slot_hot[...], NT, preferred_element_type=F32
+        )
+        return [packed[devices * q : devices * (q + 1)] for q in range(len(rows))]
+
+    def send_units(source, target, sems):
+        copies = []
+        for k in range(1, devices):
+            copy = pltpu.make_async_remote_copy(
+                src_ref=source.at[lax.rem(me + k, devices)],
+                dst_ref=target.at[k],
+                send_sem=sems.at[0, k],
+                recv_sem=sems.at[1, k],
+                device_id=any_peer(k),
+                device_id_type=MESH,
+            )
+            copy.start()
+            copies.append(copy)
+        return copies
+
+    first, second = split(jnp.where(live, unit_sums[1:2, :], 0.0))
+    local_high = (local >> 7).astype(F32)
+    local_low = (local & (LANES - 1)).astype(F32)
+    fields = pack([first, second, local_high, local_low])
+    early_send[:, 0, :] = fields[0] + fields[1]
+    early_send[:, 1, :] = fields[2]
+    early_send[:, 2, :] = fields[3]
+    early_send[:, 3, :] = jnp.zeros((devices, LANES), F32)
+    early_copies = send_units(early_send, early_in, early_sems)
+
     for k in range(1, parts):
         p = lax.rem(part_me + parts - k, parts)
         pltpu.make_async_remote_copy(
@@ -399,34 +439,9 @@
 
     lax.fori_loop(0, steps, residual_sums, 0)
 
-    unit_pair = jnp.where(live, unit_sums[0:2, :], 0.0)
-    first, second = split(unit_pair)
-    local_high = (local >> 7).astype(F32)
-    local_low = (local & (LANES - 1)).astype(F32)
-    fields = jnp.concatenate(
-        [first, local_high, local_low, second, jnp.zeros((2, blocks), F32)], axis=0
-    )
-    for o in range(0, devices, 2):
-        both = [jnp.where(owner == o + i, fields, 0.0) for i in range(2)]
-        spread[8 * o : 8 * o + 16, :] = jnp.concatenate(both, axis=0).astype(BF16)
-    packed = lax.dot_general(
-        spread[: 8 * devices, :], slot_hot[...], NT, preferred_element_type=F32
-    )
-    for o in range(devices):
-        unit_send[o] = packed[8 * o : 8 * o + 4] + packed[8 * o + 4 : 8 * o + 8]
-
-    unit_copies = []
-    for k in range(1, devices):
-        copy = pltpu.make_async_remote_copy(
-            src_ref=unit_send.at[lax.rem(me + k, devices)],
-            dst_ref=unit_in.at[k],
-            send_sem=unit_sems.at[0, k],
-            recv_sem=unit_sems.at[1, k],
-            device_id=any_peer(k),
-            device_id_type=MESH,
-        )
-        copy.start()
-        unit_copies.append(copy)
+    fields = pack(split(jnp.where(live, unit_sums[0:1, :], 0.0)))
+    unit_send[:, 0, :] = fields[0] + fields[1]
+    unit_copies = send_units(unit_send, unit_in, unit_sems)
 
     segment = segment_ref[...]
     segment_high = segment >> 7
@@ -466,48 +481,51 @@
         copy.start()
         knot_copies.append(copy)
 
-    for copy in unit_copies:
+    for copy in early_copies:
         copy.wait_recv()
-    unit_in[0] = unit_send[me]
-    unit_out[...] = jnp.concatenate([unit_in[k] for k in range(devices)], axis=1)
+    early_in[0] = early_send[me]
+    flat = jnp.concatenate([early_in[k] for k in range(devices)], axis=1)
+    flat_hot[...] = one_hot(LANES, flat[2:3].astype(jnp.int32))
+    flat_high = flat[1:2].astype(jnp.int32)
+
+    def place(value):
+        hit = lax.broadcasted_iota(jnp.int32, (unit_high, value.shape[1]), 0) == flat_high
+        halves = [jnp.where(hit, part, 0.0).astype(BF16) for part in split(value)]
+        placed = lax.dot_general(
+            jnp.concatenate(halves, axis=0), flat_hot[...], NT, preferred_element_type=F32
+        )
+        return placed[:unit_high] + placed[unit_high:]
+
+    unit_diag = place(flat[0:1])
 
     for copy in knot_copies:
         copy.wait_recv()
     total = knot_send[sky]
     for k in range(1, plane):
         total = total + knot_in[k]
-    knot_out[...] = total
-
-    for copy in fov_copies + table_copies + update_copies + unit_copies + knot_copies:
+    att_out[...] = total[0:4] / (1.0 + total[4:8])
+
+    for copy in unit_copies:
+        copy.wait_recv()
+    unit_in[0] = unit_send[me]
+    unit_right = place(jnp.concatenate([unit_in[k] for k in range(devices)], axis=1))
+    cal_out[...] = unit_right / (1.0 + unit_diag)
+
+    for copy in fov_copies + table_copies + update_copies:
         copy.wait_send()
-
-
-def finish(src_hbm, knot_hbm, unit_hbm, src_out, att_out, cal_out, knot_ref, unit_ref, sems):
-    unit_copy = pltpu.make_async_copy(unit_hbm, unit_ref, sems.at[0])
-    knot_copy = pltpu.make_async_copy(knot_hbm, knot_ref, sems.at[1])
-    src_copy = pltpu.make_async_copy(src_hbm, src_out, sems.at[2])
-    unit_copy.start()
-    knot_copy.start()
-    src_copy.start()
-    unit_copy.wait()
-    knot_copy.wait()
-    att_out[...] = knot_ref[0:4] / (1.0 + knot_ref[4:8])
-    n = cal_out.shape[0]
-    first, second = split(unit_ref[0:2])
-    flat_high = unit_ref[2:3].astype(jnp.int32)
-    flat_low = unit_ref[3:4].astype(jnp.int32)
-    high_hit = lax.broadcasted_iota(jnp.int32, (n, unit_ref.shape[1]), 0) == flat_high
-    rows = [first[0:1], second[0:1], first[1:2], second[1:2]]
-    spread_units = jnp.concatenate(
-        [jnp.where(high_hit, value, 0.0).astype(BF16) for value in rows], axis=0
-    )
-    units = lax.dot_general(
-        spread_units, one_hot(LANES, flat_low), NT, preferred_element_type=F32
-    )
-    cal_out[...] = (units[:n] + units[n : 2 * n]) / (
-        1.0 + (units[2 * n : 3 * n] + units[3 * n :])
-    )
-    src_copy.wait()
+    for copy in early_copies + unit_copies + knot_copies:
+        copy.wait_send()
+
+
+def finish(*refs):
+    count = (len(refs) - 1) // 2
+    copies = [
+        pltpu.make_async_copy(refs[i], refs[count + i], refs[-1].at[i]) for i in range(count)
+    ]
+    for copy in copies:
+        copy.start()
+    for copy in copies:
+        copy.wait()
 
 
 def shards(sizes, src, att, cal, phase, res, source, segment, unit, live):
@@ -524,13 +542,14 @@
     vmem = pl.BlockSpec(memory_space=pltpu.VMEM)
     smem = pl.BlockSpec(memory_space=pltpu.SMEM)
     dma = pltpu.SemaphoreType.DMA
-    updates, knots, units = pl.pallas_call(
+    out_shape = (
+        jax.ShapeDtypeStruct((5, SRC_DEV), F32),
+        jax.ShapeDtypeStruct((4, SEG_DEV), F32),
+        jax.ShapeDtypeStruct((CAL // devices // LANES, LANES), F32),
+    )
+    results = pl.pallas_call(
         functools.partial(kernel, sizes),
-        out_shape=(
-            jax.ShapeDtypeStruct((5, SRC_DEV), F32),
-            jax.ShapeDtypeStruct((8, SEG_DEV), F32),
-            jax.ShapeDtypeStruct((4, devices * LANES), F32),
-        ),
+        out_shape=out_shape,
         in_specs=[anywhere] * 5 + [vmem] * 3 + [smem],
         out_specs=(vmem, vmem, vmem),
         scratch_shapes=[
@@ -565,12 +584,16 @@
             pltpu.VMEM((plane, 8, SEG_DEV), F32),
             pltpu.VMEM((devices, 4, LANES), F32),
             pltpu.VMEM((devices, 4, LANES), F32),
+            pltpu.VMEM((devices, 1, LANES), F32),
+            pltpu.VMEM((devices, 1, LANES), F32),
+            pltpu.VMEM((LANES, devices * LANES), BF16),
             dma((2, steps)),
             dma((3,)),
             dma((2, n_fov)),
             dma((2, n_tm)),
             dma((2, parts)),
             dma((2, plane)),
+            dma((2, devices)),
             dma((2, devices)),
         ],
         compiler_params=pltpu.CompilerParams(
@@ -589,20 +612,12 @@
     )
     src_update, att_update, cal_update = pl.pallas_call(
         finish,
-        out_shape=(
-            jax.ShapeDtypeStruct((5, SRC_DEV), F32),
-            jax.ShapeDtypeStruct((4, SEG_DEV), F32),
-            jax.ShapeDtypeStruct((CAL // devices // LANES, LANES), F32),
-        ),
+        out_shape=out_shape,
         in_specs=[anywhere] * 3,
-        out_specs=(anywhere, vmem, vmem),
-        scratch_shapes=[
-            pltpu.VMEM(knots.shape, F32),
-            pltpu.VMEM(units.shape, F32),
-            dma((3,)),
-        ],
+        out_specs=(vmem, vmem, vmem),
+        scratch_shapes=[dma((3,))],
         compiler_params=pltpu.CompilerParams(vmem_limit_bytes=58 * 1024 * 1024),
-    )(updates, knots, units)
+    )(*results)
     return (
         src_update,
         att_update.reshape(4, 1, SEG_DEV),

time: 36.7 us -> 34.6 us (0.943)
  Pallas kernels: 35.1 us -> 33 us
    pallas_call x2, Pallas kernels: 35.1 us -> 33 us  [the longest x1 31.4 us: shards(): pl.pallas_call(functools.partial(kernel, sizes), out_shape=out_shape, in_...]
where the time goes in v4:
time: 34.6 us; the launch traced here: 34.3 us
  Pallas kernels  33 us (95%)
  between operations  1.29 us (4%)
    pallas_call x1, Pallas kernels, shards(): pl.pallas_call(functools.partial(kernel, sizes), out_shape=out_shape, in_...  31.4 us
    pallas_call x1, Pallas kernels, shards(): pl.pallas_call(finish, out_shape=out_shape, in_specs=[anywhere] * 3, out_...  1.61 us

profile of v4, /device:TPU:0, one launch (start us, length us, event | category | flops | bytes accessed | tf_op | source)
XLA Modules:
  0.0 34.3 jit_solution(2709081023961182666)
XLA Ops:
  1.3 31.4 %shard_map.112 = (f32[5,4096]{1,0:T(8,128)}, f32[4,128]{1,0:T(4,128)}, f32[128,128]{1,0:T(8,128)}) custom-call(f32[5,2048,128]{2,1,0:T(8,128)} %bitcast.8, f32[2048,4,128]{2,1,0:T(4,128)} %att_hbm.1, f32[2048,128]{1,0:T(8,128)} %cal_hbm.1, f32[2048,128]{1,0:T(8,128)} %phase_hbm.1, f32[2048,128]{1,0:T(8,128)} %res_hbm.1, s32[1,2048]{1,0:T(1,128)} %bitcast.9, ...), custom_call_target="tpu_custom_call" | custom-call | tf_op jit(solution)/shard_map/pallas_call | solution.py:550
  32.7 1.6 %shard_map.113 = (f32[5,4096]{1,0:T(8,128)}, f32[4,128]{1,0:T(4,128)}, f32[128,128]{1,0:T(8,128)}) custom-call(f32[5,4096]{1,0:T(8,128)} %get-tuple-element.9.refs_0_, f32[4,128]{1,0:T(4,128)} %get-tuple-element.10.refs_1_, f32[128,128]{1,0:T(8,128)} %get-tuple-element.11.refs_2_), custom_call_target="tpu_custom_call" | custom-call | tf_op jit(solution)/shard_map/pallas_call | solution.py:613

commit v5 on v4

--- a/solution.py
+++ b/solution.py
@@ -177,14 +177,9 @@
         pltpu.make_async_copy(phase_hbm, phase_in, whole_sems.at[2]),
     ]
 
-    def start_chunk(g, carry):
+    for g in range(min(2, steps)):
         for copy in chunk_copies(g):
             copy.start()
-        return carry
-
-    lax.fori_loop(0, steps, start_chunk, 0)
-    for copy in whole_copies:
-        copy.start()
 
     barrier = pltpu.get_barrier_semaphore()
     for k in range(1, devices):
@@ -197,9 +192,11 @@
     def group_rows(g, u):
         return pl.ds(pl.multiple_of((g * UNROLL + u) * LANES, LANES), LANES)
 
-    def source_sums(g, carry):
+    def wait_chunk(g):
         for copy in chunk_copies(g):
             copy.wait()
+
+    def source_sums(g):
         for u in range(UNROLL):
             rows = group_rows(g, u)
             for c in range(5):
@@ -212,26 +209,38 @@
                 terms = [a[i] * a[j] for i, j in index_pairs] + [a[i] * a[5] for i in range(5)]
                 totals = terms if totals is None else [x + y for x, y in zip(totals, terms)]
             sums[0:20, rows] = fold_all(folds[u], totals)
+
+    def first_steps(g, carry):
+        wait_chunk(g)
+        for copy in chunk_copies(g + 2):
+            copy.start()
+        source_sums(g)
         return carry
 
-    lax.fori_loop(0, steps, source_sums, 0)
-    sums[20:24, :] = jnp.zeros((4, blocks), F32)
+    def last_steps(g, carry):
+        wait_chunk(g)
+        source_sums(g)
+        return carry
+
+    lax.fori_loop(0, steps - 2, first_steps, 0)
+    for copy in whole_copies:
+        copy.start()
+    lax.fori_loop(steps - 2, steps, last_steps, 0)
 
     live = lax.broadcasted_iota(jnp.int32, (1, blocks), 1) < live_ref[0]
     pair = jnp.concatenate(split(jnp.where(live, sums[...], 0.0)), axis=0)
+    for h in range(0, high, 2):
+        both = [jnp.where(source_high == h + i, pair, 0.0) for i in range(2)]
+        spread[40 * h : 40 * h + 80, :] = jnp.concatenate(both, axis=0).astype(BF16)
+    placed = lax.dot_general(
+        spread[: 40 * high, :], low_hot[...], NT, preferred_element_type=F32
+    )
     for h in range(high):
-        spread[48 * h : 48 * h + 48, :] = jnp.where(source_high == h, pair, 0.0).astype(BF16)
-    placed = lax.dot_general(
-        spread[: 48 * high, :], low_hot[...], NT, preferred_element_type=F32
-    )
-    for h in range(high):
-        piece = placed[48 * h : 48 * h + 24] + placed[48 * h + 24 : 48 * h + 48]
+        piece = placed[40 * h : 40 * h + 20] + placed[40 * h + 20 : 40 * h + 40]
         p = h // per_part
         for l in range(LOW // LANES):
             row = ((h % per_part) * (LOW // LANES) + l) * 20
-            table[p // n_tm, p % n_tm, row : row + 20, :] = piece[
-                :20, l * LANES : (l + 1) * LANES
-            ]
+            table[p // n_tm, p % n_tm, row : row + 20, :] = piece[:, l * LANES : (l + 1) * LANES]
 
     pl.semaphore_wait(barrier, devices - 1)
 
@@ -537,7 +546,7 @@
     plane = n_sky * n_fov
     high = SRC_DEV // LOW
     cuts = SRC_DEV // parts // LANES
-    spread_rows = max(48 * high, 8 * devices, 64 * n_sky)
+    spread_rows = max(40 * high, 8 * devices, 64 * n_sky)
     anywhere = pl.BlockSpec(memory_space=pl.ANY)
     vmem = pl.BlockSpec(memory_space=pltpu.VMEM)
     smem = pl.BlockSpec(memory_space=pltpu.SMEM)
@@ -562,7 +571,7 @@
             pltpu.VMEM((steps, UNROLL, 4, LANES, LANES), F32),
             pltpu.VMEM((steps, UNROLL, 4, LANES, LANES), F32),
             pltpu.VMEM((steps, UNROLL, LANES, LANES), F32),
-            pltpu.VMEM((24, blocks), F32),
+            pltpu.VMEM((20, blocks), F32),
             pltpu.VMEM((32, blocks), F32),
             pltpu.VMEM((8, blocks), F32),
             pltpu.VMEM((LOW, blocks), BF16),

time: 34.6 us -> 34.7 us (level)
  no operation moved by 1% of the time
where the time goes in v5:
time: 34.7 us; the launch traced here: 34.5 us
  Pallas kernels  33.2 us (96%)
  between operations  1.29 us (4%)
    pallas_call x1, Pallas kernels, shards(): pl.pallas_call(functools.partial(kernel, sizes), out_shape=out_shape, in_...  31.6 us
    pallas_call x1, Pallas kernels, shards(): pl.pallas_call(finish, out_shape=out_shape, in_specs=[anywhere] * 3, out_...  1.61 us

profile of v5, /device:TPU:0, one launch (start us, length us, event | category | flops | bytes accessed | tf_op | source)
XLA Modules:
  0.0 34.5 jit_solution(4345520490978117354)
XLA Ops:
  1.3 31.6 %shard_map.112 = (f32[5,4096]{1,0:T(8,128)}, f32[4,128]{1,0:T(4,128)}, f32[128,128]{1,0:T(8,128)}) custom-call(f32[5,2048,128]{2,1,0:T(8,128)} %bitcast.8, f32[2048,4,128]{2,1,0:T(4,128)} %att_hbm.1, f32[2048,128]{1,0:T(8,128)} %cal_hbm.1, f32[2048,128]{1,0:T(8,128)} %phase_hbm.1, f32[2048,128]{1,0:T(8,128)} %res_hbm.1, s32[1,2048]{1,0:T(1,128)} %bitcast.9, ...), custom_call_target="tpu_custom_call" | custom-call | tf_op jit(solution)/shard_map/pallas_call | solution.py:559
  32.9 1.6 %shard_map.113 = (f32[5,4096]{1,0:T(8,128)}, f32[4,128]{1,0:T(4,128)}, f32[128,128]{1,0:T(8,128)}) custom-call(f32[5,4096]{1,0:T(8,128)} %get-tuple-element.9.refs_0_, f32[4,128]{1,0:T(4,128)} %get-tuple-element.10.refs_1_, f32[128,128]{1,0:T(8,128)} %get-tuple-element.11.refs_2_), custom_call_target="tpu_custom_call" | custom-call | tf_op jit(solution)/shard_map/pallas_call | solution.py:622
